TPU v7x, 32 devices: a whole 2x2x4 slice. The times are simulated.
32 devices in a mesh: ta: 8 (over z, y), gz: 4 (over x, core).
Axes of the slice: x: 2, y: 2, z: 4, core: 2. Of those that a mesh axis runs over, the one named last changes fastest.
Arguments:
- eigvecs: bfloat16 [8, 2, 3, 16, 256, 128], P('ta', None, None, 'gz'), may hold values from -6 to 6
- gauge_links: bfloat16 [8, 3, 3, 3, 2, 16, 256], P('ta', None, None, None, None, 'gz'), may hold values from -2.5 to 2.5
- peramb: bfloat16 [8, 4, 4, 4, 2, 128, 128], P('ta', None, 'gz'), may hold values from -0.3984375 to 0.3984375
- momenta: int32 [2, 3], replicated, may hold values from -2 to 2
- disp_paths: int32 [2, 2], replicated, may hold values from 1 to 3, as said below
- sources: int32 [4], replicated, may hold values from 0 to 7
Outputs:
- elementals: bfloat16 [8, 2, 2, 2, 128, 128], P('ta', None, None, None, 'gz')
- correlator: float32 [4, 8, 2, 2, 2], P(None, 'ta')
Inputs may be any that keep to these rules, and one draw needn't show every extreme that they name: `disp_paths`: in each momentum's row exactly one path runs along the third dimension (value 3); every other path is 1 or 2.
All inputs are finite; a program needn't handle non-finite values.
Results may differ from a plain program's by a relative error of at most 0.0081.
Values may be sent and summed in bfloat16 or wider, within the bound.
A program may use at most 128 MiB of HBM per device.

v0:
```python
import math

import jax
import jax.numpy as jnp
from jax import lax
from jax.sharding import PartitionSpec as P

LX = 16
LY = 16
NSRC = 4


HIGHEST = lax.Precision.HIGHEST


def from_behind(block, axis, distance):
    devices = range(lax.axis_size(axis))
    route = [((i - distance) % len(devices), i) for i in devices]
    return lax.ppermute(block, axis, route)


def from_root(value, axis, source):
    kept = jnp.where(lax.axis_index(axis) == source, value, 0).astype(value.dtype)
    return lax.psum(kept, axis)


def transport(link_dir, source):
    link_re = link_dir[:, :, 0].astype(jnp.float32)
    link_im = link_dir[:, :, 1].astype(jnp.float32)
    source_re = source[0].astype(jnp.float32)
    source_im = source[1].astype(jnp.float32)
    total_re = jnp.zeros(source_re.shape, jnp.float32)
    total_im = jnp.zeros(source_re.shape, jnp.float32)
    for colour in range(3):
        coef_re = link_re[:, colour][..., None]
        coef_im = link_im[:, colour][..., None]
        total_re = total_re + coef_re * source_re[colour][None] - coef_im * source_im[colour][None]
        total_im = total_im + coef_re * source_im[colour][None] + coef_im * source_re[colour][None]
    return jnp.stack([total_re, total_im])


def back_transport(link_dir, source):
    link_re = link_dir[:, :, 0].astype(jnp.float32)
    link_im = link_dir[:, :, 1].astype(jnp.float32)
    source_re = source[0].astype(jnp.float32)
    source_im = source[1].astype(jnp.float32)
    total_re = jnp.zeros(source_re.shape, jnp.float32)
    total_im = jnp.zeros(source_re.shape, jnp.float32)
    for colour in range(3):
        coef_re = link_re[colour][..., None]
        coef_im = link_im[colour][..., None]
        total_re = total_re + coef_re * source_re[colour][None] + coef_im * source_im[colour][None]
        total_im = total_im + coef_re * source_im[colour][None] - coef_im * source_re[colour][None]
    return jnp.stack([total_re, total_im])


def phase_table(momentum, zcoord, lz_total):
    xcoord = jnp.arange(LX, dtype=jnp.int32)
    ycoord = jnp.arange(LY, dtype=jnp.int32)
    volume = LX * LY * lz_total
    phase_int = (
        momentum[0] * xcoord[None, :, None] * (LY * lz_total)
        + momentum[1] * ycoord[None, None, :] * (LX * lz_total)
        + momentum[2] * zcoord[:, None, None] * (LX * LY)
    )
    phase_int = jnp.mod(phase_int, volume)
    angles = phase_int.astype(jnp.float32) * (2.0 * math.pi / volume)
    return (jnp.cos(angles), jnp.sin(angles))


def elementals_one(vectors, selected, momentum, zcoord, lz_total):
    cosine, sine_table = phase_table(momentum, zcoord, lz_total)
    cosine = cosine[None, :, :, :, None]
    sine_table = sine_table[None, :, :, :, None]
    vec_re = vectors[0].astype(jnp.float32)
    vec_im = vectors[1].astype(jnp.float32)
    phased = jnp.stack(
        [vec_re * cosine - vec_im * sine_table, -(vec_re * sine_table + vec_im * cosine)]
    ).astype(jnp.bfloat16)
    num_vec = vectors.shape[-1]
    phased_rows = phased.reshape(2, -1, num_vec)
    displaced_cols = selected.reshape(selected.shape[0], 2, -1, num_vec)
    products = lax.dot_general(
        phased_rows, displaced_cols, (((1,), (2,)), ((), ())), preferred_element_type=jnp.float32
    )
    real_part = products[0, :, :, 0] - products[1, :, :, 1]
    imag_part = products[0, :, :, 1] + products[1, :, :, 0]
    return jnp.transpose(jnp.stack([real_part, imag_part]), (2, 0, 1, 3))


def block_real(values, part_axis):
    real_half = jnp.take(values, 0, axis=part_axis)
    imag_half = jnp.take(values, 1, axis=part_axis)
    first_row = jnp.stack([real_half, imag_half], axis=part_axis)
    second_row = jnp.stack([-imag_half, real_half], axis=part_axis)
    return jnp.stack([first_row, second_row], axis=part_axis)


def contraction(sink_phi, source_phi, peramb_slice):
    peramb_block = block_real(peramb_slice, 3)
    sink_side = lax.dot_general(
        sink_phi, peramb_block, (((2, 4), (3, 5)), ((), ())), preferred_element_type=jnp.float32
    )
    source_block = block_real(source_phi, 3)
    image_side = lax.dot_general(
        peramb_slice,
        source_block,
        (((3, 5), (3, 5)), ((0,), (0,))),
        preferred_element_type=jnp.float32,
    )
    table = lax.dot_general(
        sink_side,
        image_side,
        (((4, 5, 2, 7), (1, 2, 3, 7)), ((3, 0, 1), (0, 4, 5))),
        precision=HIGHEST,
        preferred_element_type=jnp.float32,
    )
    real_sum = table[..., 0, 0] + table[..., 1, 1]
    imag_sum = table[..., 1, 0] - table[..., 0, 1]
    return jnp.stack([real_sum, imag_sum], axis=-1)


def on_device(eigvecs, gauge_links, peramb, momenta, disp_paths, sources):
    num_vec = eigvecs.shape[-1]
    z_depth = eigvecs.shape[3]
    groups = lax.axis_size("gz")
    lz_total = z_depth * groups
    row_count = num_vec // groups
    vectors = eigvecs[0].reshape(2, 3, z_depth, LX, LY, num_vec)
    links_slice = gauge_links[0].reshape(3, 3, 3, 2, z_depth, LX, LY)
    results = []
    for direction in range(2):
        axis_id = (3, 4)[direction]
        link_dir = links_slice[direction]
        shifted_up = jnp.roll(vectors, -1, axis=axis_id)
        forward = transport(link_dir, shifted_up)
        backward = back_transport(link_dir, vectors).astype(jnp.bfloat16)
        behind = jnp.roll(backward, 1, axis=axis_id).astype(jnp.float32)
        results.append((forward - behind).astype(jnp.bfloat16))
    link_dir = links_slice[2]
    top_plane = from_behind(vectors[:, :, :1], "gz", -1)
    shifted_up = jnp.concatenate([vectors[:, :, 1:], top_plane], axis=2)
    forward = transport(link_dir, shifted_up)
    backward = back_transport(link_dir, vectors).astype(jnp.bfloat16)
    bottom_plane = from_behind(backward[:, :, -1:], "gz", 1)
    behind = jnp.concatenate([bottom_plane, backward[:, :, :-1]], axis=2).astype(jnp.float32)
    results.append((forward - behind).astype(jnp.bfloat16))
    displaced = jnp.stack(results)
    zcoord = lax.axis_index("gz") * z_depth + jnp.arange(z_depth, dtype=jnp.int32)

    def one_momentum(pair):
        selected = jnp.take(displaced, pair[1] - 1, axis=0)
        return elementals_one(vectors, selected, pair[0], zcoord, lz_total)

    partial_value = lax.map(one_momentum, (momenta, disp_paths))
    norm_scale = 1.0 / math.sqrt(12.0 * LX * LY * lz_total)
    full_sum = lax.psum(partial_value, "gz")
    sink_phi = (full_sum * norm_scale).astype(jnp.bfloat16)
    rows_phi = lax.dynamic_slice_in_dim(sink_phi, lax.axis_index("gz") * row_count, row_count, 3)
    received = []
    for source_slot in range(NSRC):
        received.append(from_root(sink_phi, "ta", sources[source_slot]))
    source_phi = jnp.stack(received)
    corr_terms = contraction(sink_phi, source_phi, peramb[0])
    summed = lax.psum(corr_terms, "gz") / (8.0 * num_vec)
    return (rows_phi[None], summed[:, None])


def solution(mesh):
    placed = (
        P("ta", None, None, "gz", None, None),
        P("ta", None, None, None, None, "gz", None),
        P("ta", None, "gz", None, None, None, None),
        P(),
        P(),
        P(),
    )
    return jax.shard_map(
        on_device,
        mesh=mesh,
        in_specs=placed,
        out_specs=(P("ta", None, None, None, "gz", None), P(None, "ta", None, None, None)),
        check_vma=False,
    )
```

profile of v0, /device:TPU:0, one launch (start us, length us, event | category | flops | bytes accessed | tf_op | source)
XLA Modules:
  0.0 341.7 jit_solution(3403045023371346772)
XLA Ops:
  7.2 1.8 slice.725
  9.0 2.4 collective-permute-start
  11.4 1.7 slice_convert_fusion.1
  13.4 0.9 copy_convert_fusion
  14.7 3.4 add_convert_fusion
  18.2 0.8 pad_maximum_fusion.7
  19.3 1.0 copy_convert_fusion.4
  22.4 6.0 %add_convert_fusion.2 = (bf16[1,3,4,16,16,128]{5,4,2,1,0,3:T(8,128)(2,1)S(1)}, bf16[1,3,4,16,16,128]{5,4,2,1,0,3:T(8,128)(2,1)S(1)}, bf16[1,3,4,16,16,128]{5,4,2...) fusion(f32[3,4,16,16]{3,1,0,2:T(4,128)S(1)} %get-tuple-element.317, f32[3,4,16,16]{3,1,0,2:T(4,128)S(1)} %get-tuple-element.314, ...), kind=kLoop, calls=%fused_computation.85 | loop fusion | flops 18874368 | bytes 6438912 | tf_op jit(solution)/shard_map/convert.6
  28.6 1.2 copy-done
  30.1 0.7 slice.700
  31.0 1.1 fusion.39
  32.4 0.7 copy-done.16
  33.1 0.7 slice_bitcast_fusion.35
  34.4 1.5 fusion.37
  36.9 2.5 subtract_bitcast_fusion.2
  40.1 5.3 %subtract_bitcast_fusion.1 = (f32[1,1,3,4,16,16,128]{6,5,3,2,1,4,0:T(8,128)}, f32[1,1,3,4,16,16,128]{6,5,3,2,1,4,0:T(8,128)}) fusion(f32[3,4,16,16]{3,1,0,2:T(4,128)S(1)} %get-tuple-element.336, f32[3,4,16,16]{3,1,0,2:T(4,128)S(1)} %get-tuple-element.333, f32[3,4,16,16]{3,1,0,2:T(4,128)S(1)} %get-tuple-element.337, ...), kind=kLoop, calls=%fused_computation.83 | loop fusion | flops 8650752 | bytes 6365184 | tf_op jit(solution)/shard_map/stack | solution.py:39
  45.4 0.9 pad_maximum_fusion.8
  46.3 1.2 slice.724
  47.6 1.0 copy.302
  48.5 0.8 copy.126
  49.4 3.3 fusion.32
  52.7 1.2 fusion.45
  54.9 2.5 subtract_bitcast_fusion
  57.4 1.5 fusion.33
  59.5 3.4 copy.143
  63.0 24.4 %while.19 = (s32[]{:T(128)}, f32[2,2,2,128,128]{4,3,2,1,0:T(8,128)}, bf16[2,3,4,16,16,128]{5,4,3,2,1,0:T(8,128)(2,1)S(1)}, s32[2,3]{1,0:T(2,128)S(1)}, s32[2,2]{...) while((s32[]{:T(128)}, ...), condition=%wide.region_1.2_spmd.clone, body=%wide.region_0.1_spmd.clone.sunk | while | flops 814497152 | bytes 16014317 | solution.py:155
  63.6 1.2 multiply_multiply_fusion.3
  65.7 0.7 fusion.134
  66.4 5.0 %gather_fusion = bf16[2,2,3,4,16,16,128]{6,5,4,3,2,1,0:T(8,128)(2,1)} fusion(bf16[3,2,3,4,16,16,128]{6,5,4,3,2,1,0:T(8,128)(2,1)} %get-tuple-element.478, s32[1024]{0:T(1024)S(1)} %pad_clamp_fusion.2), kind=kCustom, calls=%fused_computation.clone.clone.1 | custom fusion | bytes 6291464 | tf_op jit(solution)/shard_map/while/body/eval_jaxpr/jit(_take)/gather | solution.py:152
  71.4 3.0 fusion.135
  74.4 0.8 copy_dynamic-update-slice_fusion.2
  75.8 1.2 multiply_multiply_fusion.3
  77.9 0.7 fusion.134
  78.6 5.0 %gather_fusion = bf16[2,2,3,4,16,16,128]{6,5,4,3,2,1,0:T(8,128)(2,1)} fusion(bf16[3,2,3,4,16,16,128]{6,5,4,3,2,1,0:T(8,128)(2,1)} %get-tuple-element.478, s32[1024]{0:T(1024)S(1)} %pad_clamp_fusion.2), kind=kCustom, calls=%fused_computation.clone.clone.1 | custom fusion | bytes 6291464 | tf_op jit(solution)/shard_map/while/body/eval_jaxpr/jit(_take)/gather | solution.py:152
  83.6 3.0 fusion.135
  86.7 0.7 copy_dynamic-update-slice_fusion.2
  90.8 31.5 %all-reduce.4.cloned.1.call-done = f32[2,2,2,128,128]{4,3,2,1,0:T(8,128)} async-done(((f32[2,2,2,128,128]{4,3,2,1,0:T(8,128)}), f32[2,2,2,128,128]{4,3,2,1,0:T(8,128)}) %all-reduce.4.cloned.1.call-update) | async-done | bytes 524304 | tf_op jit(solution)/shard_map/psum | solution.py:157
  122.3 1.9 select_bitcast_fusion
  124.1 0.9 select_bitcast_fusion.1
  126.2 4.6 %convolution_bitcast_fusion = f32[2,2,128,4,4,2,128]{6,2,5,4,3,1,0:T(8,128)} fusion(bf16[4,1,4,1,2,128,128]{6,5,3,4,2,0,1:T(8,128)(2,1)S(1)} %get-tuple-element.309, bf16[4,1,4,1,2,128,128]{6,5,3,4,2,0,1:T(8,128)(2,1)S(1)} %get-tuple-element.308, bf16[2,2,2,128,128]{4,3,2,1,0:T(8,128)(2,1)S(1)} %get-tuple-element.248), kind=kOutput, calls=%fused_computation.55 | convolution fusion | flops 1077936128 | bytes 10747904 | tf_op jit(solution)/shard_map/dot_general | solution.py:101
  130.8 74.5 %all-reduce.6.cloned.1.call-done = (bf16[1,2,2,2,128,128]{5,4,3,2,1,0:T(8,128)(2,1)}, bf16[1,2,2,2,128,128]{5,4,3,2,1,0:T(8,128)(2,1)}, bf16[1,2,2,2,128,128]{5,...) async-done(((bf16[1,2,2,2,128,128]{5,4,3,2,1,0:T(8,128)(2,1)}, bf16[1,2,2,2,128,128]{5,4,3,2,1,0:T(8,128)(2,1)}, bf16[1,2,2,2,128,128]{5,4,3,2,1,0:T(8,128)(2,1)}, ...) | async-done | bytes 1048592 | tf_op jit(solution)/shard_map/psum | solution.py:24
  205.2 1.0 constant_dynamic-update-slice_fusion.3
  206.2 1.0 constant_dynamic-update-slice_fusion.2
  207.2 1.0 constant_dynamic-update-slice_fusion.1
  208.6 4.8 %convolution_bitcast_fusion.1 = f32[4,4,128,2,2,2,128]{2,6,1,5,4,3,0:T(8,128)} fusion(bf16[1,4,1,4,2,128,128]{6,5,4,3,2,1,0:T(8,128)(2,1)S(1)} %copy-done.15, bf16[4,2,2,1,2,128,128]{6,5,2,1,0,4,3:T(8,128)(2,1)S(1)} %get-tuple-element.311, bf16[4,2,2,1,2,128,128]{6,5,2,1,0,4,3:T(8,128)(2,1)S(1)} %get-tuple-element.310), kind=kOutput, calls=%fused_computation.56 | convolution fusion | flops 1074790400 | bytes 11534336 | tf_op jit(solution)/shard_map/dot_general | solution.py:105
  213.5 13.2 %copy.151 = f32[4,4,128,2,2,2,128]{6,5,2,1,4,3,0:T(2,128)} copy(f32[4,4,128,2,2,2,128]{2,6,1,5,4,3,0:T(8,128)} %convolution_bitcast_fusion.1) | data formatting | bytes 16777216 | tf_op jit(solution)/shard_map/dot_general | solution.py:105
  226.6 100.7 %fusion.40 = f32[4,2,2,2,2]{4,3,2,1,0:T(2,128)S(1)} fusion(f32[4,4,128,2,2,2,128]{6,5,2,1,4,3,0:T(2,128)} %copy.151, f32[2,2,128,4,4,2,128]{6,2,5,4,3,1,0:T(8,128)} %convolution_bitcast_fusion), kind=kOutput, calls=%fused_computation.92 | convolution fusion | flops 50331648 | bytes 16777472 | tf_op jit(solution)/shard_map/dot_general | solution.py:111
  327.6 6.4 %psum.47 = f32[4,2,2,2]{0,2,3,1:T(2,128)S(1)} all-reduce(f32[4,2,2,2]{0,2,3,1:T(2,128)S(1)} %pad_maximum_fusion.9), channel_id=1, replica_groups=mesh['ta'=8,'gz'=4] {'gz'}, use_global_device_ids=true, to_apply=%region_7.12 | all-reduce | flops 32 | bytes 256 | tf_op jit(solution)/shard_map/psum | solution.py:165
  (126 shorter events, 13.6 us)
Async XLA Ops:
  7.2 115.1 %all-reduce.4.cloned.1.call-start = ((), (), s32[]{:S(2)}) async-start(), calls=%async_computation | async-start | bytes 1048576 | tf_op jit(solution)/shard_map/psum | solution.py:157
  9.0 4.1 %copy-start.22 = (bf16[1,3,3,3,2,4,256]{6,5,4,3,2,1,0:T(4,128)(2,1)S(1)}, bf16[1,3,3,3,2,4,256]{6,5,4,3,2,1,0:T(4,128)(2,1)}, u32[]{:S(2)}) copy-start(bf16[1,3,3,3,2,4,256]{6,5,4,3,2,1,0:T(4,128)(2,1)} %param.17) | copy-start | bytes 331780
  9.0 43.7 %collective-permute-start = (bf16[2,3,1,16,16,128]{5,4,3,2,1,0:T(8,128)(2,1)}, bf16[2,3,1,16,16,128]{5,4,3,2,1,0:T(8,128)(2,1)}, u32[]{:S(2)}, u32[]{:S(2)}) collective-permute-start(bf16[2,3,1,16,16,128]{5,4,3,2,1,0:T(8,128)(2,1)} %slice.725), channel_id=1, source_target_pairs={{1,0},{2,1},{3,2},{0,3},{5,4},{6,5},{7,6},{4,7},{9,8},{10,9},{11,1... | collective-permute-start | bytes 1179656 | tf_op jit(solution)/shard_map/ppermute | solution.py:19
  14.7 3.5 %copy-start.1 = (f32[1,1,1,4,256,128]{5,4,3,2,1,0:T(8,128)}, f32[1,1,1,4,256,128]{5,4,3,2,1,0:T(8,128)S(1)}, u32[]{:S(2)}) copy-start(f32[1,1,1,4,256,128]{5,4,3,2,1,0:T(8,128)S(1)} %get-tuple-element.288) | copy-start | bytes 1572868
  14.7 3.5 %copy-start.3 = (f32[1,1,1,4,256,128]{5,4,3,2,1,0:T(8,128)}, f32[1,1,1,4,256,128]{5,4,3,2,1,0:T(8,128)S(1)}, u32[]{:S(2)}) copy-start(f32[1,1,1,4,256,128]{5,4,3,2,1,0:T(8,128)S(1)} %get-tuple-element.289) | copy-start | bytes 1572868
  14.7 3.5 %copy-start.5 = (f32[1,1,1,4,256,128]{5,4,3,2,1,0:T(8,128)}, f32[1,1,1,4,256,128]{5,4,3,2,1,0:T(8,128)S(1)}, u32[]{:S(2)}) copy-start(f32[1,1,1,4,256,128]{5,4,3,2,1,0:T(8,128)S(1)} %get-tuple-element.290) | copy-start | bytes 1572868
  14.7 3.5 %copy-start.7 = (f32[1,1,1,4,256,128]{5,4,3,2,1,0:T(8,128)}, f32[1,1,1,4,256,128]{5,4,3,2,1,0:T(8,128)S(1)}, u32[]{:S(2)}) copy-start(f32[1,1,1,4,256,128]{5,4,3,2,1,0:T(8,128)S(1)} %get-tuple-element.383) | copy-start | bytes 1572868
  14.7 3.5 %copy-start.9 = (f32[1,1,1,4,256,128]{5,4,3,2,1,0:T(8,128)}, f32[1,1,1,4,256,128]{5,4,3,2,1,0:T(8,128)S(1)}, u32[]{:S(2)}) copy-start(f32[1,1,1,4,256,128]{5,4,3,2,1,0:T(8,128)S(1)} %get-tuple-element.384) | copy-start | bytes 1572868
  14.7 3.5 %copy-start.11 = (f32[1,1,1,4,256,128]{5,4,3,2,1,0:T(8,128)}, f32[1,1,1,4,256,128]{5,4,3,2,1,0:T(8,128)S(1)}, u32[]{:S(2)}) copy-start(f32[1,1,1,4,256,128]{5,4,3,2,1,0:T(8,128)S(1)} %get-tuple-element.385) | copy-start | bytes 1572868
  19.0 38.4 %collective-permute-start.1 = (bf16[2,3,1,16,16,128]{5,4,2,1,0,3:T(8,128)(2,1)}, bf16[2,3,1,16,16,128]{5,4,2,1,0,3:T(8,128)(2,1)}, u32[]{:S(2)}, u32[]{:S(2)}) collective-permute-start(bf16[2,3,1,16,16,128]{5,4,2,1,0,3:T(8,128)(2,1)} %pad_maximum_fusion.7), channel_id=1, source_target_pairs={{3,0},{0,1},{1,2},{2,3},{7,4},{4,5},{5,6},{6,7},{11,8},{8,9},{9,10... | collective-permute-start | bytes 1179656 | tf_op jit(solution)/shard_map/ppermute | solution.py:19
  20.6 1.0 copy-start.2
  20.6 1.2 copy-start.4
  20.6 1.3 copy-start.6
  20.6 1.5 copy-start.8
  20.6 1.6 copy-start.10
  20.7 1.8 copy-start.12
  28.4 1.4 copy-start
  30.9 1.3 copy-start.18
  31.0 1.2 copy-start.17
  32.2 1.0 copy-start.16
  49.4 3.4 copy-start.13
  54.0 0.9 copy-start.19
  54.0 0.9 copy-start.20
  54.9 2.5 copy-start.14
  59.5 3.4 %copy-start.24 = (s32[2,3]{1,0:T(2,128)S(1)}, s32[2,3]{1,0:T(2,128)}, u32[]{:S(2)}) copy-start(s32[2,3]{1,0:T(2,128)} %param.19) | copy-start | bytes 76
  59.5 3.4 %copy-start.25 = (s32[2,2]{1,0:T(2,128)S(1)}, s32[2,2]{1,0:T(2,128)}, u32[]{:S(2)}) copy-start(s32[2,2]{1,0:T(2,128)} %param.20) | copy-start | bytes 52
  63.0 24.5 %copy-start.23 = (s32[4]{0:T(128)S(1)}, s32[4]{0:T(128)}, u32[]{:S(2)}) copy-start(s32[4]{0:T(128)} %param.21) | copy-start | bytes 52
  87.4 117.8 %all-reduce.6.cloned.1.call-start = ((), (), s32[]{:S(2)}) async-start(), calls=%async_computation.1 | async-start | bytes 2097152 | tf_op jit(solution)/shard_map/psum | solution.py:24
  90.8 34.3 %copy-start.15 = (bf16[1,4,1,4,2,128,128]{6,5,4,3,2,1,0:T(8,128)(2,1)S(1)}, bf16[1,4,1,4,2,128,128]{6,5,4,3,2,1,0:T(8,128)(2,1)}, u32[]{:S(2)}) copy-start(bf16[1,4,1,4,2,128,128]{6,5,4,3,2,1,0:T(8,128)(2,1)} %param.18) | copy-start | bytes 3145732
  205.2 3.0 copy-start.21
Sparse Core Ops, SparseCore 0:
  87.5 34.6 all-reduce.3
  126.1 79.0 all-reduce.5
where the time goes:
time: 345 us; the launch traced here: 342 us
  matrix products  116 us (34%)
  waiting for transfers between devices  106 us (31%)
  other arithmetic  46.7 us (14%)
  local copies, waits for them, and re-layouts  46.4 us (13%)
  between operations  17.6 us (5%)
  blocking collectives  6.44 us (2%)
    dot_general x1, matrix products, contraction(): lax.dot_general(sink_side, image_side, (((4, 5, 2, 7), (1, 2, 3, 7)), ((3...  101 us
    psum x1, waiting for transfers between devices, from_root(): return lax.psum(kept, axis)  74.5 us
    psum x1, waiting for transfers between devices, on_device(): full_sum = lax.psum(partial_value, 'gz')  31.5 us
    dot_general x1, local copies, waits for them, and re-layouts, contraction(): lax.dot_general(peramb_slice, source_block, (((3, 5), (3, 5)), ((0,), (0,...  13.2 us
    another operation x4, other arithmetic  10.7 us
    unnamed x57, local copies, waits for them, and re-layouts  10.7 us
    another operation x3, other arithmetic, transport(): return jnp.stack([total_re, total_im])  10.4 us
    gather x2, local copies, waits for them, and re-layouts, one_momentum(): selected = jnp.take(displaced, pair[1] - 1, axis=0)  10 us
  transfers between devices with their start and end apart: 4, of which 2 were waited for; matrix products, arithmetic and copies ran while one was open for 14% of the time, Pallas kernels for 0%

commit v1 on v0

v1 whole, which is shorter than its diff:
```python
import math

import jax
import jax.numpy as jnp
from jax import lax
from jax.experimental import pallas as pl
from jax.experimental.pallas import tpu as pltpu
from jax.sharding import PartitionSpec as P

LX = 16
LY = 16
F32 = jnp.float32
BF16 = jnp.bfloat16
VMEM_BYTES = 48 * 1024 * 1024


def shifted(block, axis, distance):
    n = lax.axis_size(axis)
    return lax.ppermute(block, axis, [(i, (i + distance) % n) for i in range(n)])


def swapped(block, axis, bit):
    n = lax.axis_size(axis)
    return lax.ppermute(block, axis, [(i, i ^ bit) for i in range(n)])


def phase_angles(momenta, zcoord, lz_total):
    xcoord = jnp.arange(LX, dtype=jnp.int32)
    ycoord = jnp.arange(LY, dtype=jnp.int32)
    volume = LX * LY * lz_total
    p = momenta[:, :, None, None, None]
    phase_int = (
        p[:, 0] * xcoord[None, None, :, None] * (LY * lz_total)
        + p[:, 1] * ycoord[None, None, None, :] * (LX * lz_total)
        + p[:, 2] * zcoord[None, :, None, None] * (LX * LY)
    )
    phase_int = jnp.mod(phase_int, volume)
    return phase_int.astype(F32) * (2.0 * math.pi / volume)


def elementals_kernel(paths, turn, vec, above, top, links, phases, out, shift_buf, moved, phased, spread, total):
    z = pl.program_id(0)
    last = pl.num_programs(0) - 1

    @pl.when(z < last)
    def _():
        shift_buf[...] = above[0, :, :, 0]

    @pl.when(z == last)
    def _():
        shift_buf[...] = top[...]

    coefs = links.shape[2]
    wide = coefs * 128
    chosen = lax.broadcasted_iota(jnp.int32, (coefs, wide), 1) // 128
    row = lax.broadcasted_iota(jnp.int32, (coefs, wide), 0)
    select = jnp.where(chosen == row, 1.0, 0.0).astype(BF16)

    for direction in range(3):
        spread[...] = lax.dot_general(
            links[direction, 0], select, (((0,), (0,)), ((), ())), preferred_element_type=F32
        )

        def one_line(x1, carry, direction=direction):
            here = pl.ds(pl.multiple_of(x1 * LY, LY), LY)
            if direction == 0:
                there = pl.ds(pl.multiple_of(lax.rem(x1 + 1, LX) * LY, LY), LY)
            else:
                there = here
            source = []
            for part in range(2):
                for colour in range(3):
                    if direction == 2:
                        tile = shift_buf[part, colour, here, :].astype(F32)
                    else:
                        tile = vec[0, part, colour, 0, there, :].astype(F32)
                    if direction == 1:
                        tile = pltpu.roll(tile, LY - 1, 0)
                    source.append(tile)
            for a in range(3):
                re = None
                im = None
                for b in range(3):
                    at = (a * 3 + b) * 2
                    c_re = spread[here, at * 128:(at + 1) * 128]
                    c_im = spread[here, (at + 1) * 128:(at + 2) * 128]
                    s_re, s_im = source[b], source[3 + b]
                    t_re = c_re * s_re - c_im * s_im
                    t_im = c_re * s_im + c_im * s_re
                    re = t_re if re is None else re + t_re
                    im = t_im if im is None else im + t_im
                rows = pl.ds(pl.multiple_of(a * LX * LY + x1 * LY, LY), LY)
                moved[direction, rows, 0:128] = re.astype(BF16)
                moved[direction, rows, 128:256] = im.astype(BF16)
            return carry

        lax.fori_loop(0, LX, one_line, 0, unroll=4)

    for m in range(2):
        def one_phase(x1, carry, m=m):
            here = pl.ds(pl.multiple_of(x1 * LY, LY), LY)
            cosine = jnp.broadcast_to(phases[0, here, 2 * m:2 * m + 1], (LY, 128))
            sine = jnp.broadcast_to(phases[0, here, 2 * m + 1:2 * m + 2], (LY, 128))
            for colour in range(3):
                v_re = vec[0, 0, colour, 0, here, :].astype(F32)
                v_im = vec[0, 1, colour, 0, here, :].astype(F32)
                rc, rs, ic, js = v_re * cosine, v_re * sine, v_im * cosine, v_im * sine
                rows = pl.ds(pl.multiple_of(colour * LX * LY + x1 * LY, LY), LY)
                phased[rows, 0:128] = (rc - js).astype(BF16)
                phased[rows, 128:256] = (-(rs + ic)).astype(BF16)
                phased[rows, 256:384] = (rc + js).astype(BF16)
                phased[rows, 384:512] = (rs - ic).astype(BF16)
            return carry

        lax.fori_loop(0, LX, one_phase, 0, unroll=4)
        for k in range(2):
            prod = lax.dot_general(
                phased[...], moved[paths[m, k] - 1], (((0,), (0,)), ((), ())), preferred_element_type=F32
            )

            @pl.when(z == 0)
            def _():
                total[m, k] = prod

            @pl.when(z > 0)
            def _():
                total[m, k] += prod

    @pl.when(z == last)
    def _():
        for m in range(2):
            for k in range(2):
                d = paths[m, k] - 1
                c, s = turn[m, 2 * d], turn[m, 2 * d + 1]
                f_re = total[m, k, 0:128, 0:128] - total[m, k, 128:256, 128:256]
                f_im = total[m, k, 0:128, 128:256] + total[m, k, 128:256, 0:128]
                g_re = (total[m, k, 256:384, 0:128] - total[m, k, 384:512, 128:256]).T
                g_im = (total[m, k, 256:384, 128:256] + total[m, k, 384:512, 0:128]).T
                out[m, k, 0] = f_re - (c * g_re - s * g_im)
                out[m, k, 1] = f_im + (c * g_im + s * g_re)


def partial_elementals(eigvecs, top, links, phases, turn, paths):
    z_depth = eigvecs.shape[3]
    sites, num_vec = eigvecs.shape[4:]
    smem = pl.BlockSpec(memory_space=pltpu.SMEM)
    plane = (1, 2, 3, 1, sites, num_vec)
    return pl.pallas_call(
        elementals_kernel,
        grid=(z_depth,),
        out_shape=jax.ShapeDtypeStruct((2, 2, 2, num_vec, num_vec), F32),
        in_specs=[
            smem,
            smem,
            pl.BlockSpec(plane, lambda z: (0, 0, 0, z, 0, 0)),
            pl.BlockSpec(plane, lambda z: (0, 0, 0, jnp.minimum(z + 1, z_depth - 1), 0, 0)),
            pl.BlockSpec((2, 3, sites, num_vec), lambda z: (0, 0, 0, 0)),
            pl.BlockSpec((3, 1) + links.shape[2:], lambda z: (0, z, 0, 0)),
            pl.BlockSpec((1,) + phases.shape[1:], lambda z: (z, 0, 0)),
        ],
        out_specs=pl.BlockSpec((2, 2, 2, num_vec, num_vec), lambda z: (0, 0, 0, 0, 0)),
        scratch_shapes=[
            pltpu.VMEM((2, 3, sites, num_vec), BF16),
            pltpu.VMEM((3, 3 * sites, 2 * num_vec), BF16),
            pltpu.VMEM((3 * sites, 4 * num_vec), BF16),
            pltpu.VMEM((sites, links.shape[2] * 128), F32),
            pltpu.VMEM((2, 2, 4 * num_vec, 2 * num_vec), F32),
        ],
        compiler_params=pltpu.CompilerParams(vmem_limit_bytes=VMEM_BYTES),
        cost_estimate=pl.CostEstimate(flops=4 * 10**9, bytes_accessed=4 * 10**6, transcendentals=0),
    )(paths, turn, eigvecs, eigvecs, top, links, phases)


def correlator_kernel(sink, source, peramb, out):
    n = sink.shape[-1]
    spins = peramb.shape[1]
    tau = [(peramb[0, b, 0], peramb[0, b, 1]) for b in range(spins)]
    right = jnp.concatenate(
        [jnp.concatenate([t[0] for t in tau], axis=1), jnp.concatenate([t[1] for t in tau], axis=1)], axis=0
    )
    left = jnp.concatenate([jnp.concatenate(t, axis=1) for t in tau], axis=0)
    for mk in range(sink.shape[0]):
        f_re, f_im = sink[mk, 0], sink[mk, 1]
        block = jnp.concatenate(
            [jnp.concatenate([f_re, -f_im], axis=1), jnp.concatenate([f_im, f_re], axis=1)], axis=0
        )
        sink_side = jnp.dot(block, right, preferred_element_type=F32)
        g_re, g_im = source[0, mk, 0], source[0, mk, 1]
        block = jnp.concatenate(
            [jnp.concatenate([g_re, g_im], axis=1), jnp.concatenate([-g_im, g_re], axis=1)], axis=0
        )
        image = jnp.dot(left, block, preferred_element_type=F32)
        real = jnp.zeros((8, n), F32)
        imag = jnp.zeros((8, n), F32)
        for b in range(spins):
            s_re = sink_side[0:n, b * n:(b + 1) * n]
            s_im = sink_side[n:2 * n, b * n:(b + 1) * n]
            i_re = image[b * n:(b + 1) * n, 0:n]
            i_im = image[b * n:(b + 1) * n, n:2 * n]
            real += jnp.sum((s_re * i_re + s_im * i_im).reshape(n // 8, 8, n), axis=0)
            imag += jnp.sum((s_im * i_re - s_re * i_im).reshape(n // 8, 8, n), axis=0)
        out[0, mk, 0] = real
        out[0, mk, 1] = imag


def correlator_terms(sink, source, peramb):
    slots, spins, _, n, _ = peramb.shape
    pairs = sink.shape[0]
    return pl.pallas_call(
        correlator_kernel,
        grid=(slots,),
        out_shape=jax.ShapeDtypeStruct((slots, pairs, 2, 8, n), F32),
        in_specs=[
            pl.BlockSpec((pairs, 2, n, n), lambda s: (0, 0, 0, 0)),
            pl.BlockSpec((1, pairs, 2, n, n), lambda s: (s, 0, 0, 0, 0)),
            pl.BlockSpec((1, spins, 2, n, n), lambda s: (s, 0, 0, 0, 0)),
        ],
        out_specs=pl.BlockSpec((1, pairs, 2, 8, n), lambda s: (s, 0, 0, 0, 0)),
        compiler_params=pltpu.CompilerParams(vmem_limit_bytes=VMEM_BYTES),
        cost_estimate=pl.CostEstimate(flops=3 * 10**9, bytes_accessed=4 * 10**6, transcendentals=0),
    )(sink, source, peramb)


def gather_rows(rows):
    me = lax.axis_index("gz")
    groups = lax.axis_size("gz")
    blocks = rows[..., None, :, :]
    bit = groups // 2
    while bit:
        other = swapped(blocks, "gz", bit)
        upper = (me // bit) % 2 == 1
        low = jnp.where(upper, other, blocks)
        high = jnp.where(upper, blocks, other)
        blocks = jnp.stack([low, high], axis=-3)
        shape = blocks.shape
        blocks = blocks.reshape(shape[:-4] + (shape[-4] * 2,) + shape[-2:])
        bit //= 2
    shape = blocks.shape
    return blocks.reshape(shape[:-3] + (shape[-3] * shape[-2], shape[-1]))


def on_device(eigvecs, gauge_links, peramb, momenta, disp_paths, sources):
    num_vec = eigvecs.shape[-1]
    z_depth = eigvecs.shape[3]
    sites = eigvecs.shape[4]
    groups = lax.axis_size("gz")
    me = lax.axis_index("gz")
    lz_total = z_depth * groups
    row_count = num_vec // groups

    top = shifted(eigvecs[0, :, :, 0], "gz", -1)
    links = gauge_links[0].reshape(3, 18, z_depth, sites).transpose(0, 2, 1, 3)
    zcoord = me * z_depth + jnp.arange(z_depth, dtype=jnp.int32)
    angles = phase_angles(momenta, zcoord, lz_total).reshape(2, z_depth, sites)
    phases = jnp.stack([jnp.cos(angles), jnp.sin(angles)], axis=1)
    phases = phases.reshape(4, z_depth, sites).transpose(1, 2, 0)
    step = momenta.astype(F32) * (2.0 * math.pi / jnp.array([LX, LY, lz_total], F32))
    turn = jnp.stack([jnp.cos(step), jnp.sin(step)], axis=-1).reshape(2, 6)
    partial_value = partial_elementals(eigvecs, top, links, phases, turn, disp_paths)

    def rows_of(index):
        return lax.dynamic_slice_in_dim(partial_value, index * row_count, row_count, 3)

    full_rows = rows_of(me)
    for distance in range(1, groups):
        full_rows = full_rows + shifted(rows_of((me + distance) % groups), "gz", distance)
    norm_scale = 1.0 / math.sqrt(12.0 * LX * LY * lz_total)
    rows_phi = (full_rows * norm_scale).astype(BF16)

    slices = lax.axis_size("ta")
    if slices <= 16:
        held = jnp.stack([rows_phi] + [shifted(rows_phi, "ta", d) for d in range(1, slices)])
        chosen = jnp.mod(lax.axis_index("ta") - sources, slices)
    else:
        held = lax.all_gather(rows_phi, "ta")
        chosen = sources
    source_phi = gather_rows(jnp.take(held, chosen, axis=0))
    sink_phi = gather_rows(rows_phi)

    sink_phi = sink_phi.reshape(4, 2, num_vec, num_vec)
    source_phi = source_phi.reshape(sources.shape[0], 4, 2, num_vec, num_vec)
    terms = correlator_terms(sink_phi, source_phi, peramb[0, :, 0])
    summed = lax.psum(jnp.sum(terms, axis=(-2, -1)), "gz") / (8.0 * num_vec)
    return (rows_phi[None], summed.reshape(-1, 1, 2, 2, 2))


def solution(mesh):
    placed = (
        P("ta", None, None, "gz", None, None),
        P("ta", None, None, None, None, "gz", None),
        P("ta", None, "gz", None, None, None, None),
        P(),
        P(),
        P(),
    )
    return jax.shard_map(
        on_device,
        mesh=mesh,
        in_specs=placed,
        out_specs=(P("ta", None, None, None, "gz", None), P(None, "ta", None, None, None)),
        check_vma=False,
    )
```

time: 345 us -> 82.1 us (0.24)
  matrix products: 116 us -> 0 us
  waiting for transfers between devices: 106 us -> 17.5 us
  other arithmetic: 46.7 us -> 1.83 us
  local copies, waits for them, and re-layouts: 46.4 us -> 6.34 us
  Pallas kernels: 0 us -> 28.5 us
  starting transfers between devices: 2.46 us -> 19.4 us
  between operations: 17.6 us -> 0.95 us
    dot_general x5 -> x0, matrix products: 116 us -> none  [the longest x1 101 us: contraction(): lax.dot_general(sink_side, image_side, (((4, 5, 2, 7), (1, 2, 3, 7)), ((3...]
    psum x2 -> x0, waiting for transfers between devices: 106 us -> none  [the longest x1 74.5 us: from_root(): return lax.psum(kept, axis)]
    pallas_call x0 -> x2, Pallas kernels: none -> 28.5 us  [the longest x1 25.5 us: partial_elementals(): pl.pallas_call(elementals_kernel, grid=(z_depth,), out_shape=jax.ShapeDty...]
    another operation x15 -> x9, other arithmetic: 24.9 us -> 1.08 us  [the longest x2 0.73 us: on_device(): turn = jnp.stack([jnp.cos(step), jnp.sin(step)], axis=-1).reshape(2, 6)]
    ppermute x2 -> x15, waiting for transfers between devices: 0.01 us -> 17.5 us  [the longest x11 10.3 us: shifted(): lax.ppermute(block, axis, [(i, (i + distance) % n) for i in range(n)])]
    ppermute x2 -> x15, starting transfers between devices: 2.38 us -> 19.4 us  [the longest x11 17.2 us: shifted(): lax.ppermute(block, axis, [(i, (i + distance) % n) for i in range(n)])]
    dot_general x1 -> x0, local copies, waits for them, and re-layouts: 13.2 us -> none  [contraction(): lax.dot_general(peramb_slice, source_block, (((3, 5), (3, 5)), ((0,), (0,...]
    convert_element_type x10 -> x1, other arithmetic: 11.4 us -> 0.04 us  [on_device(): rows_phi = (full_rows * norm_scale).astype(BF16)]
  transfers between devices with their start and end apart: 4 -> 15, of which waited for: 2 -> 8; matrix products, arithmetic and copies ran while one was open for 14% -> 6% of each run, Pallas kernels for 0% -> 0%
where the time goes in v1:
time: 82.1 us; the launch traced here: 80.5 us
  Pallas kernels  28.5 us (35%)
  starting transfers between devices  19.4 us (24%)
  waiting for transfers between devices  17.5 us (21%)
  local copies, waits for them, and re-layouts  6.34 us (8%)
  blocking collectives  5.99 us (7%)
  other arithmetic  1.83 us (2%)
  between operations  0.95 us (1%)
    pallas_call x1, Pallas kernels, partial_elementals(): pl.pallas_call(elementals_kernel, grid=(z_depth,), out_shape=jax.ShapeDty...  25.5 us
    ppermute x11, starting transfers between devices, shifted(): lax.ppermute(block, axis, [(i, (i + distance) % n) for i in range(n)])  17.2 us
    ppermute x11, waiting for transfers between devices, shifted(): lax.ppermute(block, axis, [(i, (i + distance) % n) for i in range(n)])  10.3 us
    ppermute x4, waiting for transfers between devices, swapped(): return lax.ppermute(block, axis, [(i, i ^ bit) for i in range(n)])  7.22 us
    psum x1, blocking collectives, on_device(): summed = lax.psum(jnp.sum(terms, axis=(-2, -1)), 'gz') / (8.0 * num_vec)  5.99 us
    pallas_call x1, Pallas kernels, correlator_terms(): pl.pallas_call(correlator_kernel, grid=(slots,), out_shape=jax.ShapeDtype...  2.93 us
    ppermute x4, starting transfers between devices, swapped(): return lax.ppermute(block, axis, [(i, i ^ bit) for i in range(n)])  2.26 us
  transfers between devices with their start and end apart: 15, of which 8 were waited for; matrix products, arithmetic and copies ran while one was open for 6% of the time, Pallas kernels for 0%

profile of v1, /device:TPU:0, one launch (start us, length us, event | category | flops | bytes accessed | tf_op | source)
XLA Modules:
  0.0 80.5 jit_solution(3497373214129547343)
XLA Ops:
  0.6 1.1 %slice_bitcast_fusion = bf16[2,3,256,128]{3,2,1,0:T(8,128)(2,1)S(1)} fusion(bf16[1,2,3,4,256,128]{5,4,3,2,1,0:T(8,128)(2,1)} %above.1), kind=kLoop, calls=%fused_computation.5 | loop fusion | bytes 786432 | tf_op jit(solution)/shard_map/squeeze | solution.py:251
  1.8 2.4 %collective-permute-start = (bf16[2,3,256,128]{3,2,1,0:T(8,128)(2,1)S(1)}, bf16[2,3,256,128]{3,2,1,0:T(8,128)(2,1)S(1)}, u32[]{:S(2)}, u32[]{:S(2)}) collective-permute-start(bf16[2,3,256,128]{3,2,1,0:T(8,128)(2,1)S(1)} %slice_bitcast_fusion), channel_id=1, source_target_pairs={{0,3},{1,0},{2,1},{3,2},{4,7},{5,4},{6,5},{7,6},{8,11},{9,8},{10,9... | collective-permute-start | bytes 1179656 | tf_op jit(solution)/shard_map/ppermute | solution.py:19
  4.2 1.0 %slice_reduce_fusion.2 = (s32[2]{0:T(128)S(1)}, s32[2]{0:T(128)S(1)}, s32[2]{0:T(128)S(1)}) fusion(s32[2,3,1,1,1]{1,0,4,3,2:T(2,128)} %bitcast.79), kind=kLoop, calls=%fused_computation.53 | loop fusion | bytes 48 | tf_op jit(solution)/shard_map/slice | solution.py:33
  5.2 0.1 multiply_multiply_fusion.1
  5.3 0.1 broadcast_add_fusion
  5.4 0.1 add.139
  5.5 0.1 multiply_multiply_fusion
  5.5 0.2 fusion.4
  5.8 0.2 copy.30
  6.0 0.7 cosine_bitcast_fusion
  6.7 0.1 copy.27
  6.8 0.1 reshape.189.turn
  6.9 0.9 %copy.37 = bf16[3,18,4,256]{3,1,2,0:T(8,128)(2,1)S(1)} copy(bf16[3,18,4,256]{3,2,1,0:T(4,128)(2,1)} %bitcast.77) | data formatting | bytes 221184 | tf_op jit(solution)/shard_map/reshape;squeeze | solution.py:252
  7.9 1.7 %collective-permute-done.top = bf16[2,3,256,128]{3,2,1,0:T(8,128)(2,1)S(1)} collective-permute-done((bf16[2,3,256,128]{3,2,1,0:T(8,128)(2,1)S(1)}, bf16[2,3,256,128]{3,2,1,0:T(8,128)(2,1)S(1)}, u32[]{:S(2)}, u32[]{:S(2)}) %collective-permute-start) | collective-permute-done | bytes 393248 | tf_op jit(solution)/shard_map/ppermute | solution.py:19
  9.5 25.5 %shard_map.86 = f32[2,2,2,128,128]{4,3,2,1,0:T(8,128)S(1)} custom-call(s32[2,2]{1,0:T(2,128)S(1)} %copy-done.2, f32[2,6]{1,0:T(2,128)S(1)} %reshape.189.turn, bf16[1,2,3,4,256,128]{5,4,3,2,1,0:T(8,128)(2,1)S(1)} %copy-done, bf16[1,2,3,4,256,128]{5,4,3,2,1,0:T(8,128)(2,1)S(1)} %copy-done, bf16[2,3,256,128]{3,2,1,0:T(8,128)(2,1)S(1)} %collective-permute-done.top, ...), custom_call_target="tpu_custom_call" | custom-call | flops 4000000000 | bytes 4000000 | tf_op jit(solution)/shard_map/pallas_call | solution.py:148
  35.1 0.9 %collective-permute-start.1 = (f32[2,2,2,32,128]{4,3,2,1,0:T(8,128)S(1)}, f32[2,2,2,32,128]{4,3,2,1,0:T(8,128)S(1)}, u32[]{:S(2)}, u32[]{:S(2)}) collective-permute-start(f32[2,2,2,32,128]{4,3,2,1,0:T(8,128)S(1)} %get-tuple-element.11), channel_id=1, source_target_pairs={{0,1},{1,2},{2,3},{3,0},{4,5},{5,6},{6,7},{7,4},{8,9},{9,10},{10,1... | collective-permute-start | bytes 393224 | tf_op jit(solution)/shard_map/ppermute | solution.py:19
  36.0 1.5 %collective-permute-start.2 = (f32[2,2,2,32,128]{4,3,2,1,0:T(8,128)S(1)}, f32[2,2,2,32,128]{4,3,2,1,0:T(8,128)S(1)}, u32[]{:S(2)}, u32[]{:S(2)}) collective-permute-start(f32[2,2,2,32,128]{4,3,2,1,0:T(8,128)S(1)} %get-tuple-element.13), channel_id=1, source_target_pairs={{0,2},{1,3},{2,0},{3,1},{4,6},{5,7},{6,4},{7,5},{8,10},{9,11},{10,... | collective-permute-start | bytes 393224 | tf_op jit(solution)/shard_map/ppermute | solution.py:19
  37.5 2.3 %collective-permute-done.1 = f32[2,2,2,32,128]{4,3,2,1,0:T(8,128)S(1)} collective-permute-done((f32[2,2,2,32,128]{4,3,2,1,0:T(8,128)S(1)}, f32[2,2,2,32,128]{4,3,2,1,0:T(8,128)S(1)}, u32[]{:S(2)}, u32[]{:S(2)}) %collective-permute-start.1) | collective-permute-done | bytes 131104 | tf_op jit(solution)/shard_map/ppermute | solution.py:19
  39.9 2.6 %collective-permute-done.2 = f32[2,2,2,32,128]{4,3,2,1,0:T(8,128)S(1)} collective-permute-done((f32[2,2,2,32,128]{4,3,2,1,0:T(8,128)S(1)}, f32[2,2,2,32,128]{4,3,2,1,0:T(8,128)S(1)}, u32[]{:S(2)}, u32[]{:S(2)}) %collective-permute-start.2) | collective-permute-done | bytes 131104 | tf_op jit(solution)/shard_map/ppermute | solution.py:19
  42.5 1.6 %collective-permute-start.6 = (bf16[2,2,2,32,128]{4,3,2,1,0:T(8,128)(2,1)S(1)}, bf16[2,2,2,32,128]{4,3,2,1,0:T(8,128)(2,1)S(1)}, u32[]{:S(2)}, u32[]{:S(2)}) collective-permute-start(bf16[2,2,2,32,128]{4,3,2,1,0:T(8,128)(2,1)S(1)} %multiply_convert_fusion), channel_id=1, source_target_pairs={{0,4},{4,8},{8,12},{12,16},{16,20},{20,24},{24,28},{28,0},{1,5},{5... | collective-permute-start | bytes 196616 | tf_op jit(solution)/shard_map/ppermute | solution.py:19
  44.1 1.6 %collective-permute-start.7 = (bf16[2,2,2,32,128]{4,3,2,1,0:T(8,128)(2,1)S(1)}, bf16[2,2,2,32,128]{4,3,2,1,0:T(8,128)(2,1)S(1)}, u32[]{:S(2)}, u32[]{:S(2)}) collective-permute-start(bf16[2,2,2,32,128]{4,3,2,1,0:T(8,128)(2,1)S(1)} %multiply_convert_fusion), channel_id=1, source_target_pairs={{0,8},{4,12},{8,16},{12,20},{16,24},{20,28},{24,0},{28,4},{1,9},{5... | collective-permute-start | bytes 196616 | tf_op jit(solution)/shard_map/ppermute | solution.py:19
  45.6 2.5 %collective-permute-start.8 = (bf16[2,2,2,32,128]{4,3,2,1,0:T(8,128)(2,1)S(1)}, bf16[2,2,2,32,128]{4,3,2,1,0:T(8,128)(2,1)S(1)}, u32[]{:S(2)}, u32[]{:S(2)}) collective-permute-start(bf16[2,2,2,32,128]{4,3,2,1,0:T(8,128)(2,1)S(1)} %multiply_convert_fusion), channel_id=1, source_target_pairs={{0,12},{4,16},{8,20},{12,24},{16,28},{20,0},{24,4},{28,8},{1,13},{... | collective-permute-start | bytes 196616 | tf_op jit(solution)/shard_map/ppermute | solution.py:19
  48.2 1.2 %collective-permute-start.9 = (bf16[2,2,2,32,128]{4,3,2,1,0:T(8,128)(2,1)S(1)}, bf16[2,2,2,32,128]{4,3,2,1,0:T(8,128)(2,1)S(1)}, u32[]{:S(2)}, u32[]{:S(2)}) collective-permute-start(bf16[2,2,2,32,128]{4,3,2,1,0:T(8,128)(2,1)S(1)} %multiply_convert_fusion), channel_id=1, source_target_pairs={{0,16},{4,20},{8,24},{12,28},{16,0},{20,4},{24,8},{28,12},{1,17},{... | collective-permute-start | bytes 196616 | tf_op jit(solution)/shard_map/ppermute | solution.py:19
  49.4 2.6 %collective-permute-start.10 = (bf16[2,2,2,32,128]{4,3,2,1,0:T(8,128)(2,1)S(1)}, bf16[2,2,2,32,128]{4,3,2,1,0:T(8,128)(2,1)S(1)}, u32[]{:S(2)}, u32[]{:S(2)}) collective-permute-start(bf16[2,2,2,32,128]{4,3,2,1,0:T(8,128)(2,1)S(1)} %multiply_convert_fusion), channel_id=1, source_target_pairs={{0,20},{4,24},{8,28},{12,0},{16,4},{20,8},{24,12},{28,16},{1,21},{... | collective-permute-start | bytes 196616 | tf_op jit(solution)/shard_map/ppermute | solution.py:19
  52.1 1.4 %collective-permute-start.11 = (bf16[2,2,2,32,128]{4,3,2,1,0:T(8,128)(2,1)S(1)}, bf16[2,2,2,32,128]{4,3,2,1,0:T(8,128)(2,1)S(1)}, u32[]{:S(2)}, u32[]{:S(2)}) collective-permute-start(bf16[2,2,2,32,128]{4,3,2,1,0:T(8,128)(2,1)S(1)} %multiply_convert_fusion), channel_id=1, source_target_pairs={{0,24},{4,28},{8,0},{12,4},{16,8},{20,12},{24,16},{28,20},{1,25},{... | collective-permute-start | bytes 196616 | tf_op jit(solution)/shard_map/ppermute | solution.py:19
  53.4 1.5 %collective-permute-start.12 = (bf16[2,2,2,32,128]{4,3,2,1,0:T(8,128)(2,1)S(1)}, bf16[2,2,2,32,128]{4,3,2,1,0:T(8,128)(2,1)S(1)}, u32[]{:S(2)}, u32[]{:S(2)}) collective-permute-start(bf16[2,2,2,32,128]{4,3,2,1,0:T(8,128)(2,1)S(1)} %multiply_convert_fusion), channel_id=1, source_target_pairs={{0,28},{4,0},{8,4},{12,8},{16,12},{20,16},{24,20},{28,24},{1,29},{... | collective-permute-start | bytes 196616 | tf_op jit(solution)/shard_map/ppermute | solution.py:19
  54.9 1.2 %collective-permute-done.8 = bf16[2,2,2,32,128]{4,3,2,1,0:T(8,128)(2,1)S(1)} collective-permute-done((bf16[2,2,2,32,128]{4,3,2,1,0:T(8,128)(2,1)S(1)}, bf16[2,2,2,32,128]{4,3,2,1,0:T(8,128)(2,1)S(1)}, u32[]{:S(2)}, u32[]{:S(2)}) %collective-permute-start.8) | collective-permute-done | bytes 65568 | tf_op jit(solution)/shard_map/ppermute | solution.py:19
  56.1 0.9 %collective-permute-start.4 = (bf16[2,2,2,1,32,128]{5,4,2,1,0,3:T(8,128)(2,1)S(1)}, bf16[2,2,2,1,32,128]{5,4,2,1,0,3:T(8,128)(2,1)S(1)}, u32[]{:S(2)}, u32[]{:S(2)}) collective-permute-start(bf16[2,2,2,1,32,128]{5,4,2,1,0,3:T(8,128)(2,1)S(1)} %bitcast.75), channel_id=1, source_target_pairs={{0,2},{1,3},{2,0},{3,1},{4,6},{5,7},{6,4},{7,5},{8,10},{9,11},{10,... | collective-permute-start | bytes 196616 | tf_op jit(solution)/shard_map/ppermute | solution.py:24
  57.1 0.5 collective-permute-done.9
  57.6 2.0 %collective-permute-done.11 = bf16[2,2,2,32,128]{4,3,2,1,0:T(8,128)(2,1)S(1)} collective-permute-done((bf16[2,2,2,32,128]{4,3,2,1,0:T(8,128)(2,1)S(1)}, bf16[2,2,2,32,128]{4,3,2,1,0:T(8,128)(2,1)S(1)}, u32[]{:S(2)}, u32[]{:S(2)}) %collective-permute-start.11) | collective-permute-done | bytes 65568 | tf_op jit(solution)/shard_map/ppermute | solution.py:19
  59.6 0.6 gather_fusion
  60.2 0.1 bitcast_select_fusion
  60.3 0.7 collective-permute-start.13
  61.1 5.7 %collective-permute-done.13 = bf16[4,2,2,2,1,32,128]{6,5,3,2,1,0,4:T(8,128)(2,1)S(1)} collective-permute-done((bf16[4,2,2,2,1,32,128]{6,5,3,2,1,0,4:T(8,128)(2,1)S(1)}, bf16[4,2,2,2,1,32,128]{6,5,3,2,1,0,4:T(8,128)(2,1)S(1)}, u32[]{:S(2)}, u32[]{:S(2)}) %collective-permute-start.13) | collective-permute-done | bytes 262176 | tf_op jit(solution)/shard_map/ppermute | solution.py:24
  66.8 0.1 select_bitcast_fusion.3
  66.9 0.1 maximum_bitcast_fusion
  66.9 0.1 collective-permute-start.14
  67.0 0.6 collective-permute-start.5
  67.6 1.5 %collective-permute-done.5 = bf16[2,2,2,2,32,128]{5,4,2,1,0,3:T(8,128)(2,1)S(1)} collective-permute-done((bf16[2,2,2,2,32,128]{5,4,2,1,0,3:T(8,128)(2,1)S(1)}, bf16[2,2,2,2,32,128]{5,4,2,1,0,3:T(8,128)(2,1)S(1)}, u32[]{:S(2)}, u32[]{:S(2)}) %collective-permute-start.5) | collective-permute-done | bytes 131104 | tf_op jit(solution)/shard_map/ppermute | solution.py:24
  69.2 0.1 select_bitcast_fusion.1
  69.3 0.1 pad_maximum_fusion
  69.4 0.1 copy.32
  69.6 1.1 %copy-done.1 = bf16[1,4,1,4,2,128,128]{6,5,4,3,2,1,0:T(8,128)(2,1)S(1)} copy-done((bf16[1,4,1,4,2,128,128]{6,5,4,3,2,1,0:T(8,128)(2,1)S(1)}, bf16[1,4,1,4,2,128,128]{6,5,4,3,2,1,0:T(8,128)(2,1)}, u32[]{:S(2)}) %copy-start.1) | copy-done | bytes 1048600
  70.6 2.9 %shard_map.87 = f32[4,4,2,8,128]{4,3,2,1,0:T(8,128)S(1)} custom-call(bf16[4,2,128,128]{3,2,1,0:T(8,128)(2,1)S(1)} %bitcast.72, bf16[4,4,2,128,128]{4,3,2,1,0:T(8,128)(2,1)S(1)} %bitcast.70, bf16[4,4,2,128,128]{4,3,2,1,0:T(8,128)(2,1)S(1)} %bitcast.74), custom_call_target="tpu_custom_call" | custom-call | flops 3000000000 | bytes 4000000 | tf_op jit(solution)/shard_map/pallas_call | solution.py:209
  73.6 0.1 reduce_sum.9
  73.7 0.1 copy.33
  73.8 6.0 %psum.7 = f32[4,4,2]{1,0,2:T(4,128)S(1)} all-reduce(f32[4,4,2]{1,0,2:T(4,128)S(1)} %copy.33), channel_id=1, replica_groups=mesh['ta'=8,'gz'=4] {'gz'}, use_global_device_ids=true, to_apply=%region_1.2 | all-reduce | flops 32 | bytes 256 | tf_op jit(solution)/shard_map/psum | solution.py:283
  79.8 0.7 copy.34
  (38 shorter events, 0.4 us)
Async XLA Ops:
  0.6 8.9 %copy-start = (bf16[1,2,3,4,256,128]{5,4,3,2,1,0:T(8,128)(2,1)S(1)}, bf16[1,2,3,4,256,128]{5,4,3,2,1,0:T(8,128)(2,1)}, u32[]{:S(2)}) copy-start(bf16[1,2,3,4,256,128]{5,4,3,2,1,0:T(8,128)(2,1)} %above.1) | copy-start | bytes 4718596
  0.6 8.9 %copy-start.2 = (s32[2,2]{1,0:T(2,128)S(1)}, s32[2,2]{1,0:T(2,128)}, u32[]{:S(2)}) copy-start(s32[2,2]{1,0:T(2,128)} %paths.1) | copy-start | bytes 52
  1.8 7.7 %collective-permute-start = (bf16[2,3,256,128]{3,2,1,0:T(8,128)(2,1)S(1)}, bf16[2,3,256,128]{3,2,1,0:T(8,128)(2,1)S(1)}, u32[]{:S(2)}, u32[]{:S(2)}) collective-permute-start(bf16[2,3,256,128]{3,2,1,0:T(8,128)(2,1)S(1)} %slice_bitcast_fusion), channel_id=1, source_target_pairs={{0,3},{1,0},{2,1},{3,2},{4,7},{5,4},{6,5},{7,6},{8,11},{9,8},{10,9... | collective-permute-start | bytes 1179656 | tf_op jit(solution)/shard_map/ppermute | solution.py:19
  9.5 28.0 %copy-start.4 = (s32[4]{0:T(128)S(1)}, s32[4]{0:T(128)}, u32[]{:S(2)}) copy-start(s32[4]{0:T(128)} %param.12) | copy-start | bytes 52
  35.1 4.7 %collective-permute-start.1 = (f32[2,2,2,32,128]{4,3,2,1,0:T(8,128)S(1)}, f32[2,2,2,32,128]{4,3,2,1,0:T(8,128)S(1)}, u32[]{:S(2)}, u32[]{:S(2)}) collective-permute-start(f32[2,2,2,32,128]{4,3,2,1,0:T(8,128)S(1)} %get-tuple-element.11), channel_id=1, source_target_pairs={{0,1},{1,2},{2,3},{3,0},{4,5},{5,6},{6,7},{7,4},{8,9},{9,10},{10,1... | collective-permute-start | bytes 393224 | tf_op jit(solution)/shard_map/ppermute | solution.py:19
  36.0 6.4 %collective-permute-start.2 = (f32[2,2,2,32,128]{4,3,2,1,0:T(8,128)S(1)}, f32[2,2,2,32,128]{4,3,2,1,0:T(8,128)S(1)}, u32[]{:S(2)}, u32[]{:S(2)}) collective-permute-start(f32[2,2,2,32,128]{4,3,2,1,0:T(8,128)S(1)} %get-tuple-element.13), channel_id=1, source_target_pairs={{0,2},{1,3},{2,0},{3,1},{4,6},{5,7},{6,4},{7,5},{8,10},{9,11},{10,... | collective-permute-start | bytes 393224 | tf_op jit(solution)/shard_map/ppermute | solution.py:19
  37.5 4.9 %collective-permute-start.3 = (f32[2,2,2,32,128]{4,3,2,1,0:T(8,128)S(1)}, f32[2,2,2,32,128]{4,3,2,1,0:T(8,128)S(1)}, u32[]{:S(2)}, u32[]{:S(2)}) collective-permute-start(f32[2,2,2,32,128]{4,3,2,1,0:T(8,128)S(1)} %get-tuple-element.12), channel_id=1, source_target_pairs={{0,3},{1,0},{2,1},{3,2},{4,7},{5,4},{6,5},{7,6},{8,11},{9,8},{10,9... | collective-permute-start | bytes 393224 | tf_op jit(solution)/shard_map/ppermute | solution.py:19
  42.5 24.4 %copy-start.3 = (bf16[2,2,2,32,128]{4,3,2,1,0:T(8,128)(2,1)}, bf16[2,2,2,32,128]{4,3,2,1,0:T(8,128)(2,1)S(1)}, u32[]{:S(2)}) copy-start(bf16[2,2,2,32,128]{4,3,2,1,0:T(8,128)(2,1)S(1)} %multiply_convert_fusion) | copy-start | bytes 196612
  42.5 9.6 %collective-permute-start.6 = (bf16[2,2,2,32,128]{4,3,2,1,0:T(8,128)(2,1)S(1)}, bf16[2,2,2,32,128]{4,3,2,1,0:T(8,128)(2,1)S(1)}, u32[]{:S(2)}, u32[]{:S(2)}) collective-permute-start(bf16[2,2,2,32,128]{4,3,2,1,0:T(8,128)(2,1)S(1)} %multiply_convert_fusion), channel_id=1, source_target_pairs={{0,4},{4,8},{8,12},{12,16},{16,20},{20,24},{24,28},{28,0},{1,5},{5... | collective-permute-start | bytes 196616 | tf_op jit(solution)/shard_map/ppermute | solution.py:19
  44.1 9.4 %collective-permute-start.7 = (bf16[2,2,2,32,128]{4,3,2,1,0:T(8,128)(2,1)S(1)}, bf16[2,2,2,32,128]{4,3,2,1,0:T(8,128)(2,1)S(1)}, u32[]{:S(2)}, u32[]{:S(2)}) collective-permute-start(bf16[2,2,2,32,128]{4,3,2,1,0:T(8,128)(2,1)S(1)} %multiply_convert_fusion), channel_id=1, source_target_pairs={{0,8},{4,12},{8,16},{12,20},{16,24},{20,28},{24,0},{28,4},{1,9},{5... | collective-permute-start | bytes 196616 | tf_op jit(solution)/shard_map/ppermute | solution.py:19
  45.6 10.5 %collective-permute-start.8 = (bf16[2,2,2,32,128]{4,3,2,1,0:T(8,128)(2,1)S(1)}, bf16[2,2,2,32,128]{4,3,2,1,0:T(8,128)(2,1)S(1)}, u32[]{:S(2)}, u32[]{:S(2)}) collective-permute-start(bf16[2,2,2,32,128]{4,3,2,1,0:T(8,128)(2,1)S(1)} %multiply_convert_fusion), channel_id=1, source_target_pairs={{0,12},{4,16},{8,20},{12,24},{16,28},{20,0},{24,4},{28,8},{1,13},{... | collective-permute-start | bytes 196616 | tf_op jit(solution)/shard_map/ppermute | solution.py:19
  48.2 9.4 %collective-permute-start.9 = (bf16[2,2,2,32,128]{4,3,2,1,0:T(8,128)(2,1)S(1)}, bf16[2,2,2,32,128]{4,3,2,1,0:T(8,128)(2,1)S(1)}, u32[]{:S(2)}, u32[]{:S(2)}) collective-permute-start(bf16[2,2,2,32,128]{4,3,2,1,0:T(8,128)(2,1)S(1)} %multiply_convert_fusion), channel_id=1, source_target_pairs={{0,16},{4,20},{8,24},{12,28},{16,0},{20,4},{24,8},{28,12},{1,17},{... | collective-permute-start | bytes 196616 | tf_op jit(solution)/shard_map/ppermute | solution.py:19
  49.4 8.1 %collective-permute-start.10 = (bf16[2,2,2,32,128]{4,3,2,1,0:T(8,128)(2,1)S(1)}, bf16[2,2,2,32,128]{4,3,2,1,0:T(8,128)(2,1)S(1)}, u32[]{:S(2)}, u32[]{:S(2)}) collective-permute-start(bf16[2,2,2,32,128]{4,3,2,1,0:T(8,128)(2,1)S(1)} %multiply_convert_fusion), channel_id=1, source_target_pairs={{0,20},{4,24},{8,28},{12,0},{16,4},{20,8},{24,12},{28,16},{1,21},{... | collective-permute-start | bytes 196616 | tf_op jit(solution)/shard_map/ppermute | solution.py:19
  52.1 7.5 %collective-permute-start.11 = (bf16[2,2,2,32,128]{4,3,2,1,0:T(8,128)(2,1)S(1)}, bf16[2,2,2,32,128]{4,3,2,1,0:T(8,128)(2,1)S(1)}, u32[]{:S(2)}, u32[]{:S(2)}) collective-permute-start(bf16[2,2,2,32,128]{4,3,2,1,0:T(8,128)(2,1)S(1)} %multiply_convert_fusion), channel_id=1, source_target_pairs={{0,24},{4,28},{8,0},{12,4},{16,8},{20,12},{24,16},{28,20},{1,25},{... | collective-permute-start | bytes 196616 | tf_op jit(solution)/shard_map/ppermute | solution.py:19
  53.4 6.2 %collective-permute-start.12 = (bf16[2,2,2,32,128]{4,3,2,1,0:T(8,128)(2,1)S(1)}, bf16[2,2,2,32,128]{4,3,2,1,0:T(8,128)(2,1)S(1)}, u32[]{:S(2)}, u32[]{:S(2)}) collective-permute-start(bf16[2,2,2,32,128]{4,3,2,1,0:T(8,128)(2,1)S(1)} %multiply_convert_fusion), channel_id=1, source_target_pairs={{0,28},{4,0},{8,4},{12,8},{16,12},{20,16},{24,20},{28,24},{1,29},{... | collective-permute-start | bytes 196616 | tf_op jit(solution)/shard_map/ppermute | solution.py:19
  56.1 4.9 %collective-permute-start.4 = (bf16[2,2,2,1,32,128]{5,4,2,1,0,3:T(8,128)(2,1)S(1)}, bf16[2,2,2,1,32,128]{5,4,2,1,0,3:T(8,128)(2,1)S(1)}, u32[]{:S(2)}, u32[]{:S(2)}) collective-permute-start(bf16[2,2,2,1,32,128]{5,4,2,1,0,3:T(8,128)(2,1)S(1)} %bitcast.75), channel_id=1, source_target_pairs={{0,2},{1,3},{2,0},{3,1},{4,6},{5,7},{6,4},{7,5},{8,10},{9,11},{10,... | collective-permute-start | bytes 196616 | tf_op jit(solution)/shard_map/ppermute | solution.py:24
  60.3 6.4 %collective-permute-start.13 = (bf16[4,2,2,2,1,32,128]{6,5,3,2,1,0,4:T(8,128)(2,1)S(1)}, bf16[4,2,2,2,1,32,128]{6,5,3,2,1,0,4:T(8,128)(2,1)S(1)}, u32[]{:S(2)}, u32[]{:S(2)}) collective-permute-start(bf16[4,2,2,2,1,32,128]{6,5,3,2,1,0,4:T(8,128)(2,1)S(1)} %bitcast_select_fusion), channel_id=1, source_target_pairs={{0,2},{1,3},{2,0},{3,1},{4,6},{5,7},{6,4},{7,5},{8,10},{9,11},{10,... | collective-permute-start | bytes 786440 | tf_op jit(solution)/shard_map/ppermute | solution.py:24
  66.9 2.3 %collective-permute-start.14 = (bf16[4,2,2,2,2,32,128]{6,5,3,2,1,0,4:T(8,128)(2,1)S(1)}, bf16[4,2,2,2,2,32,128]{6,5,3,2,1,0,4:T(8,128)(2,1)S(1)}, u32[]{:S(2)}, u32[]{:S(2)}) collective-permute-start(bf16[4,2,2,2,2,32,128]{6,5,3,2,1,0,4:T(8,128)(2,1)S(1)} %maximum_bitcast_fusion), channel_id=1, source_target_pairs={{0,1},{1,0},{2,3},{3,2},{4,5},{5,4},{6,7},{7,6},{8,9},{9,8},{10,11... | collective-permute-start | bytes 1572872 | tf_op jit(solution)/shard_map/ppermute | solution.py:24
  67.0 2.1 %collective-permute-start.5 = (bf16[2,2,2,2,32,128]{5,4,2,1,0,3:T(8,128)(2,1)S(1)}, bf16[2,2,2,2,32,128]{5,4,2,1,0,3:T(8,128)(2,1)S(1)}, u32[]{:S(2)}, u32[]{:S(2)}) collective-permute-start(bf16[2,2,2,2,32,128]{5,4,2,1,0,3:T(8,128)(2,1)S(1)} %maximum_bitcast_fusion.1), channel_id=1, source_target_pairs={{0,1},{1,0},{2,3},{3,2},{4,5},{5,4},{6,7},{7,6},{8,9},{9,8},{10,11... | collective-permute-start | bytes 393224 | tf_op jit(solution)/shard_map/ppermute | solution.py:24
  69.4 1.2 %copy-start.1 = (bf16[1,4,1,4,2,128,128]{6,5,4,3,2,1,0:T(8,128)(2,1)S(1)}, bf16[1,4,1,4,2,128,128]{6,5,4,3,2,1,0:T(8,128)(2,1)}, u32[]{:S(2)}) copy-start(bf16[1,4,1,4,2,128,128]{6,5,4,3,2,1,0:T(8,128)(2,1)} %param.9) | copy-start | bytes 3145732

commit v2 on v1

--- a/solution.py
+++ b/solution.py
@@ -11,6 +11,7 @@
 LY = 16
 F32 = jnp.float32
 BF16 = jnp.bfloat16
+UNROLL = 16
 VMEM_BYTES = 48 * 1024 * 1024
 
 
@@ -38,17 +39,35 @@
     return phase_int.astype(F32) * (2.0 * math.pi / volume)
 
 
-def elementals_kernel(paths, turn, vec, above, top, links, phases, out, shift_buf, moved, phased, spread, total):
+def transport_plane(source_at, spread, moved, slot):
+    def one_line(x1, carry):
+        here = pl.ds(pl.multiple_of(x1 * LY, LY), LY)
+        source = source_at(x1)
+        for a in range(3):
+            re = None
+            im = None
+            for b in range(3):
+                at = (a * 3 + b) * 2
+                c_re = spread[here, at * 128:(at + 1) * 128]
+                c_im = spread[here, (at + 1) * 128:(at + 2) * 128]
+                s_re, s_im = source[b], source[3 + b]
+                t_re = c_re * s_re - c_im * s_im
+                t_im = c_re * s_im + c_im * s_re
+                re = t_re if re is None else re + t_re
+                im = t_im if im is None else im + t_im
+            rows = pl.ds(pl.multiple_of(a * LX * LY + x1 * LY, LY), LY)
+            moved[slot, rows, 0:128] = re.astype(BF16)
+            moved[slot, rows, 128:256] = im.astype(BF16)
+        return carry
+
+    lax.fori_loop(0, LX, one_line, 0, unroll=UNROLL)
+
+
+def elementals_kernel(paths, turn, vec, above, top, links, phases, out, moved, phased, spread, total):
     z = pl.program_id(0)
     last = pl.num_programs(0) - 1
-
-    @pl.when(z < last)
-    def _():
-        shift_buf[...] = above[0, :, :, 0]
-
-    @pl.when(z == last)
-    def _():
-        shift_buf[...] = top[...]
+    at_top = z == last
+    in_plane = [paths[m, 0] + paths[m, 1] - 4 for m in range(2)]
 
     coefs = links.shape[2]
     wide = coefs * 128
@@ -56,86 +75,78 @@
     row = lax.broadcasted_iota(jnp.int32, (coefs, wide), 0)
     select = jnp.where(chosen == row, 1.0, 0.0).astype(BF16)
 
-    for direction in range(3):
-        spread[...] = lax.dot_general(
+    def spread_links(slot, direction):
+        spread[slot] = lax.dot_general(
             links[direction, 0], select, (((0,), (0,)), ((), ())), preferred_element_type=F32
         )
 
-        def one_line(x1, carry, direction=direction):
-            here = pl.ds(pl.multiple_of(x1 * LY, LY), LY)
-            if direction == 0:
-                there = pl.ds(pl.multiple_of(lax.rem(x1 + 1, LX) * LY, LY), LY)
-            else:
-                there = here
-            source = []
-            for part in range(2):
-                for colour in range(3):
-                    if direction == 2:
-                        tile = shift_buf[part, colour, here, :].astype(F32)
-                    else:
-                        tile = vec[0, part, colour, 0, there, :].astype(F32)
-                    if direction == 1:
-                        tile = pltpu.roll(tile, LY - 1, 0)
-                    source.append(tile)
-            for a in range(3):
-                re = None
-                im = None
-                for b in range(3):
-                    at = (a * 3 + b) * 2
-                    c_re = spread[here, at * 128:(at + 1) * 128]
-                    c_im = spread[here, (at + 1) * 128:(at + 2) * 128]
-                    s_re, s_im = source[b], source[3 + b]
-                    t_re = c_re * s_re - c_im * s_im
-                    t_im = c_re * s_im + c_im * s_re
-                    re = t_re if re is None else re + t_re
-                    im = t_im if im is None else im + t_im
-                rows = pl.ds(pl.multiple_of(a * LX * LY + x1 * LY, LY), LY)
-                moved[direction, rows, 0:128] = re.astype(BF16)
-                moved[direction, rows, 128:256] = im.astype(BF16)
-            return carry
-
-        lax.fori_loop(0, LX, one_line, 0, unroll=4)
-
+    def next_plane(x1):
+        here = pl.ds(pl.multiple_of(x1 * LY, LY), LY)
+        return [
+            jnp.where(at_top, top[part, colour, here, :], above[0, part, colour, 0, here, :]).astype(F32)
+            for part in range(2)
+            for colour in range(3)
+        ]
+
+    def next_in_plane(direction):
+        along_first = jnp.where(direction == 0, 1, 0)
+        turned = jnp.where(direction == 0, 0, LY - 1)
+
+        def source_at(x1):
+            line = lax.rem(x1 + along_first, LX)
+            there = pl.ds(pl.multiple_of(line * LY, LY), LY)
+            return [
+                pltpu.roll(vec[0, part, colour, 0, there, :].astype(F32), turned, 0)
+                for part in range(2)
+                for colour in range(3)
+            ]
+
+        return source_at
+
+    def add_product(slot, lhs, rhs):
+        prod = jnp.dot(lhs, rhs, preferred_element_type=F32)
+        total[slot] = jnp.where(z == 0, prod, total[slot] + prod)
+
+    sites = LX * LY
+    for colour in range(3):
+        v_re = vec[0, 0, colour, 0].astype(F32).T
+        v_im = vec[0, 1, colour, 0].astype(F32).T
+        columns = slice(colour * sites, (colour + 1) * sites)
+        for m in range(2):
+            cosine = phases[0, 2 * m:2 * m + 1, :]
+            sine = phases[0, 2 * m + 1:2 * m + 2, :]
+            rc, rs, ic, js = v_re * cosine, v_re * sine, v_im * cosine, v_im * sine
+            phased[m, 0:128, columns] = (rc - js).astype(BF16)
+            phased[m, 128:256, columns] = (-(rs + ic)).astype(BF16)
+            phased[m, 256:384, columns] = (rc + js).astype(BF16)
+            phased[m, 384:512, columns] = (rs - ic).astype(BF16)
+
+    spread_links(2, 2)
+    spread_links(0, in_plane[0])
+    transport_plane(next_plane, spread.at[2], moved, 2)
     for m in range(2):
-        def one_phase(x1, carry, m=m):
-            here = pl.ds(pl.multiple_of(x1 * LY, LY), LY)
-            cosine = jnp.broadcast_to(phases[0, here, 2 * m:2 * m + 1], (LY, 128))
-            sine = jnp.broadcast_to(phases[0, here, 2 * m + 1:2 * m + 2], (LY, 128))
-            for colour in range(3):
-                v_re = vec[0, 0, colour, 0, here, :].astype(F32)
-                v_im = vec[0, 1, colour, 0, here, :].astype(F32)
-                rc, rs, ic, js = v_re * cosine, v_re * sine, v_im * cosine, v_im * sine
-                rows = pl.ds(pl.multiple_of(colour * LX * LY + x1 * LY, LY), LY)
-                phased[rows, 0:128] = (rc - js).astype(BF16)
-                phased[rows, 128:256] = (-(rs + ic)).astype(BF16)
-                phased[rows, 256:384] = (rc + js).astype(BF16)
-                phased[rows, 384:512] = (rs - ic).astype(BF16)
-            return carry
-
-        lax.fori_loop(0, LX, one_phase, 0, unroll=4)
-        for k in range(2):
-            prod = lax.dot_general(
-                phased[...], moved[paths[m, k] - 1], (((0,), (0,)), ((), ())), preferred_element_type=F32
-            )
-
-            @pl.when(z == 0)
-            def _():
-                total[m, k] = prod
-
-            @pl.when(z > 0)
-            def _():
-                total[m, k] += prod
+        add_product(2 + m, phased[m], moved[2])
+    transport_plane(next_in_plane(in_plane[0]), spread.at[0], moved, 0)
+    add_product(0, phased[0], moved[0])
+
+    @pl.when(in_plane[1] != in_plane[0])
+    def _():
+        spread_links(1, in_plane[1])
+        transport_plane(next_in_plane(in_plane[1]), spread.at[1], moved, 1)
+
+    add_product(1, phased[1], moved[jnp.where(in_plane[1] != in_plane[0], 1, 0)])
 
     @pl.when(z == last)
     def _():
         for m in range(2):
             for k in range(2):
                 d = paths[m, k] - 1
+                slot = jnp.where(d == 2, 2 + m, m)
                 c, s = turn[m, 2 * d], turn[m, 2 * d + 1]
-                f_re = total[m, k, 0:128, 0:128] - total[m, k, 128:256, 128:256]
-                f_im = total[m, k, 0:128, 128:256] + total[m, k, 128:256, 0:128]
-                g_re = (total[m, k, 256:384, 0:128] - total[m, k, 384:512, 128:256]).T
-                g_im = (total[m, k, 256:384, 128:256] + total[m, k, 384:512, 0:128]).T
+                f_re = total[slot, 0:128, 0:128] - total[slot, 128:256, 128:256]
+                f_im = total[slot, 0:128, 128:256] + total[slot, 128:256, 0:128]
+                g_re = (total[slot, 256:384, 0:128] - total[slot, 384:512, 128:256]).T
+                g_im = (total[slot, 256:384, 128:256] + total[slot, 384:512, 0:128]).T
                 out[m, k, 0] = f_re - (c * g_re - s * g_im)
                 out[m, k, 1] = f_im + (c * g_im + s * g_re)
 
@@ -160,11 +171,10 @@
         ],
         out_specs=pl.BlockSpec((2, 2, 2, num_vec, num_vec), lambda z: (0, 0, 0, 0, 0)),
         scratch_shapes=[
-            pltpu.VMEM((2, 3, sites, num_vec), BF16),
             pltpu.VMEM((3, 3 * sites, 2 * num_vec), BF16),
-            pltpu.VMEM((3 * sites, 4 * num_vec), BF16),
-            pltpu.VMEM((sites, links.shape[2] * 128), F32),
-            pltpu.VMEM((2, 2, 4 * num_vec, 2 * num_vec), F32),
+            pltpu.VMEM((2, 4 * num_vec, 3 * sites), BF16),
+            pltpu.VMEM((3, sites, links.shape[2] * 128), F32),
+            pltpu.VMEM((4, 4 * num_vec, 2 * num_vec), F32),
         ],
         compiler_params=pltpu.CompilerParams(vmem_limit_bytes=VMEM_BYTES),
         cost_estimate=pl.CostEstimate(flops=4 * 10**9, bytes_accessed=4 * 10**6, transcendentals=0),
@@ -253,7 +263,7 @@
     zcoord = me * z_depth + jnp.arange(z_depth, dtype=jnp.int32)
     angles = phase_angles(momenta, zcoord, lz_total).reshape(2, z_depth, sites)
     phases = jnp.stack([jnp.cos(angles), jnp.sin(angles)], axis=1)
-    phases = phases.reshape(4, z_depth, sites).transpose(1, 2, 0)
+    phases = phases.reshape(4, z_depth, sites).transpose(1, 0, 2)
     step = momenta.astype(F32) * (2.0 * math.pi / jnp.array([LX, LY, lz_total], F32))
     turn = jnp.stack([jnp.cos(step), jnp.sin(step)], axis=-1).reshape(2, 6)
     partial_value = partial_elementals(eigvecs, top, links, phases, turn, disp_paths)

time: 82.1 us -> 69.2 us (0.84)
  the two profiles are of different devices: /device:TPU:0 before, /device:TPU:14 now
where the time goes in v2:
time: 69.2 us; the launch traced here: 68.9 us
  waiting for transfers between devices  20.9 us (30%)
  starting transfers between devices  16.7 us (24%)
  Pallas kernels  13.6 us (20%)
  local copies, waits for them, and re-layouts  8.09 us (12%)
  blocking collectives  6.88 us (10%)
  other arithmetic  1.82 us (3%)
  between operations  0.94 us (1%)
    ppermute x11, starting transfers between devices, shifted(): lax.ppermute(block, axis, [(i, (i + distance) % n) for i in range(n)])  13.8 us
    ppermute x11, waiting for transfers between devices, shifted(): lax.ppermute(block, axis, [(i, (i + distance) % n) for i in range(n)])  12.6 us
    pallas_call x1, Pallas kernels, partial_elementals(): pl.pallas_call(elementals_kernel, grid=(z_depth,), out_shape=jax.ShapeDty...  10.7 us
    ppermute x4, waiting for transfers between devices, swapped(): return lax.ppermute(block, axis, [(i, i ^ bit) for i in range(n)])  8.26 us
    psum x1, blocking collectives, on_device(): summed = lax.psum(jnp.sum(terms, axis=(-2, -1)), 'gz') / (8.0 * num_vec)  6.88 us
    unnamed x17, local copies, waits for them, and re-layouts  3.25 us
    pallas_call x1, Pallas kernels, correlator_terms(): pl.pallas_call(correlator_kernel, grid=(slots,), out_shape=jax.ShapeDtype...  2.92 us
    ppermute x4, starting transfers between devices, swapped(): return lax.ppermute(block, axis, [(i, i ^ bit) for i in range(n)])  2.87 us
  transfers between devices with their start and end apart: 15, of which 10 were waited for; matrix products, arithmetic and copies ran while one was open for 6% of the time, Pallas kernels for 0%

profile of v2, /device:TPU:14, one launch (start us, length us, event | category | flops | bytes accessed | tf_op | source)
XLA Modules:
  0.0 68.9 jit_solution(9152376376575554432)
XLA Ops:
  0.6 1.0 %slice_bitcast_fusion = bf16[2,3,256,128]{3,2,1,0:T(8,128)(2,1)S(1)} fusion(bf16[1,2,3,4,256,128]{5,4,3,2,1,0:T(8,128)(2,1)} %above.1), kind=kLoop, calls=%fused_computation.5 | loop fusion | bytes 786432 | tf_op jit(solution)/shard_map/squeeze | solution.py:261
  1.7 1.0 %slice_reduce_fusion.2 = (s32[2]{0:T(128)S(1)}, s32[2]{0:T(128)S(1)}, s32[2]{0:T(128)S(1)}) fusion(s32[2,3,1,1,1]{1,0,4,3,2:T(2,128)} %bitcast.81), kind=kLoop, calls=%fused_computation.54 | loop fusion | bytes 48 | tf_op jit(solution)/shard_map/slice | solution.py:34
  2.7 0.1 multiply_multiply_fusion.1
  2.8 0.1 broadcast_add_fusion
  2.9 0.1 add.139
  3.1 0.2 fusion.4
  3.3 0.7 %cosine_bitcast_fusion = (f32[2,3,1]{1,0,2:T(2,128)S(1)}, f32[2,3,1]{1,0,2:T(2,128)S(1)}) fusion(s32[2,3]{1,0:T(2,128)} %param.10), kind=kLoop, calls=%fused_computation.56 | loop fusion | flops 12 | bytes 72 | tf_op jit(solution)/shard_map/stack | solution.py:268
  4.0 0.1 copy.25
  4.1 0.1 reshape.189.turn
  4.2 0.9 %copy.37 = bf16[3,18,4,256]{3,1,2,0:T(8,128)(2,1)S(1)} copy(bf16[3,18,4,256]{3,2,1,0:T(4,128)(2,1)} %bitcast.79) | data formatting | bytes 221184 | tf_op jit(solution)/shard_map/reshape;squeeze | solution.py:262
  5.2 1.9 %collective-permute-done.top = bf16[2,3,256,128]{3,2,1,0:T(8,128)(2,1)S(1)} collective-permute-done((bf16[2,3,256,128]{3,2,1,0:T(8,128)(2,1)S(1)}, bf16[2,3,256,128]{3,2,1,0:T(8,128)(2,1)S(1)}, u32[]{:S(2)}, u32[]{:S(2)}) %collective-permute-start) | collective-permute-done | bytes 393248 | tf_op jit(solution)/shard_map/ppermute | solution.py:20
  7.0 1.4 %copy-done = bf16[1,2,3,4,256,128]{5,4,3,2,1,0:T(8,128)(2,1)S(1)} copy-done((bf16[1,2,3,4,256,128]{5,4,3,2,1,0:T(8,128)(2,1)S(1)}, bf16[1,2,3,4,256,128]{5,4,3,2,1,0:T(8,128)(2,1)}, u32[]{:S(2)}) %copy-start) | copy-done | bytes 1572888
  8.4 0.7 copy-done.2
  9.1 10.7 %shard_map.86 = f32[2,2,2,128,128]{4,3,2,1,0:T(8,128)S(1)} custom-call(s32[2,2]{1,0:T(2,128)S(1)} %copy-done.2, f32[2,6]{1,0:T(2,128)S(1)} %reshape.189.turn, bf16[1,2,3,4,256,128]{5,4,3,2,1,0:T(8,128)(2,1)S(1)} %copy-done, bf16[1,2,3,4,256,128]{5,4,3,2,1,0:T(8,128)(2,1)S(1)} %copy-done, bf16[2,3,256,128]{3,2,1,0:T(8,128)(2,1)S(1)} %collective-permute-done.top, ...), custom_call_target="tpu_custom_call" | custom-call | flops 4000000000 | bytes 4000000 | tf_op jit(solution)/shard_map/pallas_call | solution.py:159
  19.8 1.8 %collective-permute-start.1 = (f32[2,2,2,32,128]{4,3,2,1,0:T(8,128)S(1)}, f32[2,2,2,32,128]{4,3,2,1,0:T(8,128)S(1)}, u32[]{:S(2)}, u32[]{:S(2)}) collective-permute-start(f32[2,2,2,32,128]{4,3,2,1,0:T(8,128)S(1)} %get-tuple-element.11), channel_id=1, source_target_pairs={{0,1},{1,2},{2,3},{3,0},{4,5},{5,6},{6,7},{7,4},{8,9},{9,10},{10,1... | collective-permute-start | bytes 393224 | tf_op jit(solution)/shard_map/ppermute | solution.py:20
  21.6 0.6 collective-permute-start.2
  22.2 0.9 %collective-permute-start.3 = (f32[2,2,2,32,128]{4,3,2,1,0:T(8,128)S(1)}, f32[2,2,2,32,128]{4,3,2,1,0:T(8,128)S(1)}, u32[]{:S(2)}, u32[]{:S(2)}) collective-permute-start(f32[2,2,2,32,128]{4,3,2,1,0:T(8,128)S(1)} %get-tuple-element.12), channel_id=1, source_target_pairs={{0,3},{1,0},{2,1},{3,2},{4,7},{5,4},{6,5},{7,6},{8,11},{9,8},{10,9... | collective-permute-start | bytes 393224 | tf_op jit(solution)/shard_map/ppermute | solution.py:20
  23.1 1.4 %collective-permute-done.1 = f32[2,2,2,32,128]{4,3,2,1,0:T(8,128)S(1)} collective-permute-done((f32[2,2,2,32,128]{4,3,2,1,0:T(8,128)S(1)}, f32[2,2,2,32,128]{4,3,2,1,0:T(8,128)S(1)}, u32[]{:S(2)}, u32[]{:S(2)}) %collective-permute-start.1) | collective-permute-done | bytes 131104 | tf_op jit(solution)/shard_map/ppermute | solution.py:20
  24.5 2.8 %collective-permute-done.2 = f32[2,2,2,32,128]{4,3,2,1,0:T(8,128)S(1)} collective-permute-done((f32[2,2,2,32,128]{4,3,2,1,0:T(8,128)S(1)}, f32[2,2,2,32,128]{4,3,2,1,0:T(8,128)S(1)}, u32[]{:S(2)}, u32[]{:S(2)}) %collective-permute-start.2) | collective-permute-done | bytes 131104 | tf_op jit(solution)/shard_map/ppermute | solution.py:20
  27.3 0.4 collective-permute-done.3
  27.7 1.6 %collective-permute-start.6 = (bf16[2,2,2,32,128]{4,3,2,1,0:T(8,128)(2,1)S(1)}, bf16[2,2,2,32,128]{4,3,2,1,0:T(8,128)(2,1)S(1)}, u32[]{:S(2)}, u32[]{:S(2)}) collective-permute-start(bf16[2,2,2,32,128]{4,3,2,1,0:T(8,128)(2,1)S(1)} %multiply_convert_fusion), channel_id=1, source_target_pairs={{0,4},{4,8},{8,12},{12,16},{16,20},{20,24},{24,28},{28,0},{1,5},{5... | collective-permute-start | bytes 196616 | tf_op jit(solution)/shard_map/ppermute | solution.py:20
  29.3 1.6 %collective-permute-start.7 = (bf16[2,2,2,32,128]{4,3,2,1,0:T(8,128)(2,1)S(1)}, bf16[2,2,2,32,128]{4,3,2,1,0:T(8,128)(2,1)S(1)}, u32[]{:S(2)}, u32[]{:S(2)}) collective-permute-start(bf16[2,2,2,32,128]{4,3,2,1,0:T(8,128)(2,1)S(1)} %multiply_convert_fusion), channel_id=1, source_target_pairs={{0,8},{4,12},{8,16},{12,20},{16,24},{20,28},{24,0},{28,4},{1,9},{5... | collective-permute-start | bytes 196616 | tf_op jit(solution)/shard_map/ppermute | solution.py:20
  30.9 1.2 %collective-permute-start.8 = (bf16[2,2,2,32,128]{4,3,2,1,0:T(8,128)(2,1)S(1)}, bf16[2,2,2,32,128]{4,3,2,1,0:T(8,128)(2,1)S(1)}, u32[]{:S(2)}, u32[]{:S(2)}) collective-permute-start(bf16[2,2,2,32,128]{4,3,2,1,0:T(8,128)(2,1)S(1)} %multiply_convert_fusion), channel_id=1, source_target_pairs={{0,12},{4,16},{8,20},{12,24},{16,28},{20,0},{24,4},{28,8},{1,13},{... | collective-permute-start | bytes 196616 | tf_op jit(solution)/shard_map/ppermute | solution.py:20
  32.0 1.7 %collective-permute-start.9 = (bf16[2,2,2,32,128]{4,3,2,1,0:T(8,128)(2,1)S(1)}, bf16[2,2,2,32,128]{4,3,2,1,0:T(8,128)(2,1)S(1)}, u32[]{:S(2)}, u32[]{:S(2)}) collective-permute-start(bf16[2,2,2,32,128]{4,3,2,1,0:T(8,128)(2,1)S(1)} %multiply_convert_fusion), channel_id=1, source_target_pairs={{0,16},{4,20},{8,24},{12,28},{16,0},{20,4},{24,8},{28,12},{1,17},{... | collective-permute-start | bytes 196616 | tf_op jit(solution)/shard_map/ppermute | solution.py:20
  33.7 1.3 %collective-permute-start.10 = (bf16[2,2,2,32,128]{4,3,2,1,0:T(8,128)(2,1)S(1)}, bf16[2,2,2,32,128]{4,3,2,1,0:T(8,128)(2,1)S(1)}, u32[]{:S(2)}, u32[]{:S(2)}) collective-permute-start(bf16[2,2,2,32,128]{4,3,2,1,0:T(8,128)(2,1)S(1)} %multiply_convert_fusion), channel_id=1, source_target_pairs={{0,20},{4,24},{8,28},{12,0},{16,4},{20,8},{24,12},{28,16},{1,21},{... | collective-permute-start | bytes 196616 | tf_op jit(solution)/shard_map/ppermute | solution.py:20
  35.0 1.3 %collective-permute-start.11 = (bf16[2,2,2,32,128]{4,3,2,1,0:T(8,128)(2,1)S(1)}, bf16[2,2,2,32,128]{4,3,2,1,0:T(8,128)(2,1)S(1)}, u32[]{:S(2)}, u32[]{:S(2)}) collective-permute-start(bf16[2,2,2,32,128]{4,3,2,1,0:T(8,128)(2,1)S(1)} %multiply_convert_fusion), channel_id=1, source_target_pairs={{0,24},{4,28},{8,0},{12,4},{16,8},{20,12},{24,16},{28,20},{1,25},{... | collective-permute-start | bytes 196616 | tf_op jit(solution)/shard_map/ppermute | solution.py:20
  36.4 1.9 %collective-permute-start.12 = (bf16[2,2,2,32,128]{4,3,2,1,0:T(8,128)(2,1)S(1)}, bf16[2,2,2,32,128]{4,3,2,1,0:T(8,128)(2,1)S(1)}, u32[]{:S(2)}, u32[]{:S(2)}) collective-permute-start(bf16[2,2,2,32,128]{4,3,2,1,0:T(8,128)(2,1)S(1)} %multiply_convert_fusion), channel_id=1, source_target_pairs={{0,28},{4,0},{8,4},{12,8},{16,12},{20,16},{24,20},{28,24},{1,29},{... | collective-permute-start | bytes 196616 | tf_op jit(solution)/shard_map/ppermute | solution.py:20
  38.3 2.0 %collective-permute-done.8 = bf16[2,2,2,32,128]{4,3,2,1,0:T(8,128)(2,1)S(1)} collective-permute-done((bf16[2,2,2,32,128]{4,3,2,1,0:T(8,128)(2,1)S(1)}, bf16[2,2,2,32,128]{4,3,2,1,0:T(8,128)(2,1)S(1)}, u32[]{:S(2)}, u32[]{:S(2)}) %collective-permute-start.8) | collective-permute-done | bytes 65568 | tf_op jit(solution)/shard_map/ppermute | solution.py:20
  40.4 0.7 %collective-permute-start.4 = (bf16[2,2,2,1,32,128]{5,4,2,1,0,3:T(8,128)(2,1)S(1)}, bf16[2,2,2,1,32,128]{5,4,2,1,0,3:T(8,128)(2,1)S(1)}, u32[]{:S(2)}, u32[]{:S(2)}) collective-permute-start(bf16[2,2,2,1,32,128]{5,4,2,1,0,3:T(8,128)(2,1)S(1)} %bitcast.77), channel_id=1, source_target_pairs={{0,2},{1,3},{2,0},{3,1},{4,6},{5,7},{6,4},{7,5},{8,10},{9,11},{10,... | collective-permute-start | bytes 196616 | tf_op jit(solution)/shard_map/ppermute | solution.py:25
  41.1 0.4 collective-permute-done.9
  41.5 1.9 %collective-permute-done.11 = bf16[2,2,2,32,128]{4,3,2,1,0:T(8,128)(2,1)S(1)} collective-permute-done((bf16[2,2,2,32,128]{4,3,2,1,0:T(8,128)(2,1)S(1)}, bf16[2,2,2,32,128]{4,3,2,1,0:T(8,128)(2,1)S(1)}, u32[]{:S(2)}, u32[]{:S(2)}) %collective-permute-start.11) | collective-permute-done | bytes 65568 | tf_op jit(solution)/shard_map/ppermute | solution.py:20
  43.4 1.9 %collective-permute-done.12 = bf16[2,2,2,32,128]{4,3,2,1,0:T(8,128)(2,1)S(1)} collective-permute-done((bf16[2,2,2,32,128]{4,3,2,1,0:T(8,128)(2,1)S(1)}, bf16[2,2,2,32,128]{4,3,2,1,0:T(8,128)(2,1)S(1)}, u32[]{:S(2)}, u32[]{:S(2)}) %collective-permute-start.12) | collective-permute-done | bytes 65568 | tf_op jit(solution)/shard_map/ppermute | solution.py:20
  45.3 0.6 gather_fusion
  45.9 0.1 bitcast_select_fusion
  46.0 1.5 %collective-permute-start.13 = (bf16[4,2,2,2,1,32,128]{6,5,3,2,1,0,4:T(8,128)(2,1)S(1)}, bf16[4,2,2,2,1,32,128]{6,5,3,2,1,0,4:T(8,128)(2,1)S(1)}, u32[]{:S(2)}, u32[]{:S(2)}) collective-permute-start(bf16[4,2,2,2,1,32,128]{6,5,3,2,1,0,4:T(8,128)(2,1)S(1)} %bitcast_select_fusion), channel_id=1, source_target_pairs={{0,2},{1,3},{2,0},{3,1},{4,6},{5,7},{6,4},{7,5},{8,10},{9,11},{10,... | collective-permute-start | bytes 786440 | tf_op jit(solution)/shard_map/ppermute | solution.py:25
  47.6 6.8 %collective-permute-done.13 = bf16[4,2,2,2,1,32,128]{6,5,3,2,1,0,4:T(8,128)(2,1)S(1)} collective-permute-done((bf16[4,2,2,2,1,32,128]{6,5,3,2,1,0,4:T(8,128)(2,1)S(1)}, bf16[4,2,2,2,1,32,128]{6,5,3,2,1,0,4:T(8,128)(2,1)S(1)}, u32[]{:S(2)}, u32[]{:S(2)}) %collective-permute-start.13) | collective-permute-done | bytes 262176 | tf_op jit(solution)/shard_map/ppermute | solution.py:25
  54.3 0.1 select_bitcast_fusion.3
  54.6 0.6 collective-permute-start.5
  55.2 1.5 %collective-permute-done.5 = bf16[2,2,2,2,32,128]{5,4,2,1,0,3:T(8,128)(2,1)S(1)} collective-permute-done((bf16[2,2,2,2,32,128]{5,4,2,1,0,3:T(8,128)(2,1)S(1)}, bf16[2,2,2,2,32,128]{5,4,2,1,0,3:T(8,128)(2,1)S(1)}, u32[]{:S(2)}, u32[]{:S(2)}) %collective-permute-start.5) | collective-permute-done | bytes 131104 | tf_op jit(solution)/shard_map/ppermute | solution.py:25
  56.8 0.1 select_bitcast_fusion.1
  56.8 0.1 pad_maximum_fusion
  57.0 0.1 copy.30
  57.1 1.1 %copy-done.1 = bf16[1,4,1,4,2,128,128]{6,5,4,3,2,1,0:T(8,128)(2,1)S(1)} copy-done((bf16[1,4,1,4,2,128,128]{6,5,4,3,2,1,0:T(8,128)(2,1)S(1)}, bf16[1,4,1,4,2,128,128]{6,5,4,3,2,1,0:T(8,128)(2,1)}, u32[]{:S(2)}) %copy-start.1) | copy-done | bytes 1048600
  58.2 2.9 %shard_map.87 = f32[4,4,2,8,128]{4,3,2,1,0:T(8,128)S(1)} custom-call(bf16[4,2,128,128]{3,2,1,0:T(8,128)(2,1)S(1)} %bitcast.73, bf16[4,4,2,128,128]{4,3,2,1,0:T(8,128)(2,1)S(1)} %bitcast.72, bf16[4,4,2,128,128]{4,3,2,1,0:T(8,128)(2,1)S(1)} %bitcast.76), custom_call_target="tpu_custom_call" | custom-call | flops 3000000000 | bytes 4000000 | tf_op jit(solution)/shard_map/pallas_call | solution.py:219
  61.1 0.1 reduce_sum.9
  61.2 0.1 copy.31
  61.3 6.9 %psum.7 = f32[4,4,2]{1,0,2:T(4,128)S(1)} all-reduce(f32[4,4,2]{1,0,2:T(4,128)S(1)} %copy.31), channel_id=1, replica_groups=mesh['ta'=8,'gz'=4] {'gz'}, use_global_device_ids=true, to_apply=%region_1.2 | all-reduce | flops 32 | bytes 256 | tf_op jit(solution)/shard_map/psum | solution.py:293
  68.2 0.7 copy.32
  (38 shorter events, 0.6 us)
Async XLA Ops:
  1.7 5.4 %collective-permute-start = (bf16[2,3,256,128]{3,2,1,0:T(8,128)(2,1)S(1)}, bf16[2,3,256,128]{3,2,1,0:T(8,128)(2,1)S(1)}, u32[]{:S(2)}, u32[]{:S(2)}) collective-permute-start(bf16[2,3,256,128]{3,2,1,0:T(8,128)(2,1)S(1)} %slice_bitcast_fusion), channel_id=1, source_target_pairs={{0,3},{1,0},{2,1},{3,2},{4,7},{5,4},{6,5},{7,6},{8,11},{9,8},{10,9... | collective-permute-start | bytes 1179656 | tf_op jit(solution)/shard_map/ppermute | solution.py:20
  7.0 1.4 %copy-start = (bf16[1,2,3,4,256,128]{5,4,3,2,1,0:T(8,128)(2,1)S(1)}, bf16[1,2,3,4,256,128]{5,4,3,2,1,0:T(8,128)(2,1)}, u32[]{:S(2)}) copy-start(bf16[1,2,3,4,256,128]{5,4,3,2,1,0:T(8,128)(2,1)} %above.1) | copy-start | bytes 4718596
  8.4 0.7 copy-start.2
  9.1 14.0 %copy-start.4 = (s32[4]{0:T(128)S(1)}, s32[4]{0:T(128)}, u32[]{:S(2)}) copy-start(s32[4]{0:T(128)} %param.12) | copy-start | bytes 52
  19.8 4.6 %collective-permute-start.1 = (f32[2,2,2,32,128]{4,3,2,1,0:T(8,128)S(1)}, f32[2,2,2,32,128]{4,3,2,1,0:T(8,128)S(1)}, u32[]{:S(2)}, u32[]{:S(2)}) collective-permute-start(f32[2,2,2,32,128]{4,3,2,1,0:T(8,128)S(1)} %get-tuple-element.11), channel_id=1, source_target_pairs={{0,1},{1,2},{2,3},{3,0},{4,5},{5,6},{6,7},{7,4},{8,9},{9,10},{10,1... | collective-permute-start | bytes 393224 | tf_op jit(solution)/shard_map/ppermute | solution.py:20
  21.6 5.6 %collective-permute-start.2 = (f32[2,2,2,32,128]{4,3,2,1,0:T(8,128)S(1)}, f32[2,2,2,32,128]{4,3,2,1,0:T(8,128)S(1)}, u32[]{:S(2)}, u32[]{:S(2)}) collective-permute-start(f32[2,2,2,32,128]{4,3,2,1,0:T(8,128)S(1)} %get-tuple-element.13), channel_id=1, source_target_pairs={{0,2},{1,3},{2,0},{3,1},{4,6},{5,7},{6,4},{7,5},{8,10},{9,11},{10,... | collective-permute-start | bytes 393224 | tf_op jit(solution)/shard_map/ppermute | solution.py:20
  22.2 5.4 %collective-permute-start.3 = (f32[2,2,2,32,128]{4,3,2,1,0:T(8,128)S(1)}, f32[2,2,2,32,128]{4,3,2,1,0:T(8,128)S(1)}, u32[]{:S(2)}, u32[]{:S(2)}) collective-permute-start(f32[2,2,2,32,128]{4,3,2,1,0:T(8,128)S(1)} %get-tuple-element.12), channel_id=1, source_target_pairs={{0,3},{1,0},{2,1},{3,2},{4,7},{5,4},{6,5},{7,6},{8,11},{9,8},{10,9... | collective-permute-start | bytes 393224 | tf_op jit(solution)/shard_map/ppermute | solution.py:20
  27.7 26.7 %copy-start.3 = (bf16[2,2,2,32,128]{4,3,2,1,0:T(8,128)(2,1)}, bf16[2,2,2,32,128]{4,3,2,1,0:T(8,128)(2,1)S(1)}, u32[]{:S(2)}) copy-start(bf16[2,2,2,32,128]{4,3,2,1,0:T(8,128)(2,1)S(1)} %multiply_convert_fusion) | copy-start | bytes 196612
  27.7 7.3 %collective-permute-start.6 = (bf16[2,2,2,32,128]{4,3,2,1,0:T(8,128)(2,1)S(1)}, bf16[2,2,2,32,128]{4,3,2,1,0:T(8,128)(2,1)S(1)}, u32[]{:S(2)}, u32[]{:S(2)}) collective-permute-start(bf16[2,2,2,32,128]{4,3,2,1,0:T(8,128)(2,1)S(1)} %multiply_convert_fusion), channel_id=1, source_target_pairs={{0,4},{4,8},{8,12},{12,16},{16,20},{20,24},{24,28},{28,0},{1,5},{5... | collective-permute-start | bytes 196616 | tf_op jit(solution)/shard_map/ppermute | solution.py:20
  29.3 7.1 %collective-permute-start.7 = (bf16[2,2,2,32,128]{4,3,2,1,0:T(8,128)(2,1)S(1)}, bf16[2,2,2,32,128]{4,3,2,1,0:T(8,128)(2,1)S(1)}, u32[]{:S(2)}, u32[]{:S(2)}) collective-permute-start(bf16[2,2,2,32,128]{4,3,2,1,0:T(8,128)(2,1)S(1)} %multiply_convert_fusion), channel_id=1, source_target_pairs={{0,8},{4,12},{8,16},{12,20},{16,24},{20,28},{24,0},{28,4},{1,9},{5... | collective-permute-start | bytes 196616 | tf_op jit(solution)/shard_map/ppermute | solution.py:20
  30.9 9.5 %collective-permute-start.8 = (bf16[2,2,2,32,128]{4,3,2,1,0:T(8,128)(2,1)S(1)}, bf16[2,2,2,32,128]{4,3,2,1,0:T(8,128)(2,1)S(1)}, u32[]{:S(2)}, u32[]{:S(2)}) collective-permute-start(bf16[2,2,2,32,128]{4,3,2,1,0:T(8,128)(2,1)S(1)} %multiply_convert_fusion), channel_id=1, source_target_pairs={{0,12},{4,16},{8,20},{12,24},{16,28},{20,0},{24,4},{28,8},{1,13},{... | collective-permute-start | bytes 196616 | tf_op jit(solution)/shard_map/ppermute | solution.py:20
  32.0 9.4 %collective-permute-start.9 = (bf16[2,2,2,32,128]{4,3,2,1,0:T(8,128)(2,1)S(1)}, bf16[2,2,2,32,128]{4,3,2,1,0:T(8,128)(2,1)S(1)}, u32[]{:S(2)}, u32[]{:S(2)}) collective-permute-start(bf16[2,2,2,32,128]{4,3,2,1,0:T(8,128)(2,1)S(1)} %multiply_convert_fusion), channel_id=1, source_target_pairs={{0,16},{4,20},{8,24},{12,28},{16,0},{20,4},{24,8},{28,12},{1,17},{... | collective-permute-start | bytes 196616 | tf_op jit(solution)/shard_map/ppermute | solution.py:20
  33.7 7.8 %collective-permute-start.10 = (bf16[2,2,2,32,128]{4,3,2,1,0:T(8,128)(2,1)S(1)}, bf16[2,2,2,32,128]{4,3,2,1,0:T(8,128)(2,1)S(1)}, u32[]{:S(2)}, u32[]{:S(2)}) collective-permute-start(bf16[2,2,2,32,128]{4,3,2,1,0:T(8,128)(2,1)S(1)} %multiply_convert_fusion), channel_id=1, source_target_pairs={{0,20},{4,24},{8,28},{12,0},{16,4},{20,8},{24,12},{28,16},{1,21},{... | collective-permute-start | bytes 196616 | tf_op jit(solution)/shard_map/ppermute | solution.py:20
  35.0 8.4 %collective-permute-start.11 = (bf16[2,2,2,32,128]{4,3,2,1,0:T(8,128)(2,1)S(1)}, bf16[2,2,2,32,128]{4,3,2,1,0:T(8,128)(2,1)S(1)}, u32[]{:S(2)}, u32[]{:S(2)}) collective-permute-start(bf16[2,2,2,32,128]{4,3,2,1,0:T(8,128)(2,1)S(1)} %multiply_convert_fusion), channel_id=1, source_target_pairs={{0,24},{4,28},{8,0},{12,4},{16,8},{20,12},{24,16},{28,20},{1,25},{... | collective-permute-start | bytes 196616 | tf_op jit(solution)/shard_map/ppermute | solution.py:20
  36.4 8.9 %collective-permute-start.12 = (bf16[2,2,2,32,128]{4,3,2,1,0:T(8,128)(2,1)S(1)}, bf16[2,2,2,32,128]{4,3,2,1,0:T(8,128)(2,1)S(1)}, u32[]{:S(2)}, u32[]{:S(2)}) collective-permute-start(bf16[2,2,2,32,128]{4,3,2,1,0:T(8,128)(2,1)S(1)} %multiply_convert_fusion), channel_id=1, source_target_pairs={{0,28},{4,0},{8,4},{12,8},{16,12},{20,16},{24,20},{28,24},{1,29},{... | collective-permute-start | bytes 196616 | tf_op jit(solution)/shard_map/ppermute | solution.py:20
  40.4 7.2 %collective-permute-start.4 = (bf16[2,2,2,1,32,128]{5,4,2,1,0,3:T(8,128)(2,1)S(1)}, bf16[2,2,2,1,32,128]{5,4,2,1,0,3:T(8,128)(2,1)S(1)}, u32[]{:S(2)}, u32[]{:S(2)}) collective-permute-start(bf16[2,2,2,1,32,128]{5,4,2,1,0,3:T(8,128)(2,1)S(1)} %bitcast.77), channel_id=1, source_target_pairs={{0,2},{1,3},{2,0},{3,1},{4,6},{5,7},{6,4},{7,5},{8,10},{9,11},{10,... | collective-permute-start | bytes 196616 | tf_op jit(solution)/shard_map/ppermute | solution.py:25
  46.0 8.3 %collective-permute-start.13 = (bf16[4,2,2,2,1,32,128]{6,5,3,2,1,0,4:T(8,128)(2,1)S(1)}, bf16[4,2,2,2,1,32,128]{6,5,3,2,1,0,4:T(8,128)(2,1)S(1)}, u32[]{:S(2)}, u32[]{:S(2)}) collective-permute-start(bf16[4,2,2,2,1,32,128]{6,5,3,2,1,0,4:T(8,128)(2,1)S(1)} %bitcast_select_fusion), channel_id=1, source_target_pairs={{0,2},{1,3},{2,0},{3,1},{4,6},{5,7},{6,4},{7,5},{8,10},{9,11},{10,... | collective-permute-start | bytes 786440 | tf_op jit(solution)/shard_map/ppermute | solution.py:25
  54.5 2.3 %collective-permute-start.14 = (bf16[4,2,2,2,2,32,128]{6,5,3,2,1,0,4:T(8,128)(2,1)S(1)}, bf16[4,2,2,2,2,32,128]{6,5,3,2,1,0,4:T(8,128)(2,1)S(1)}, u32[]{:S(2)}, u32[]{:S(2)}) collective-permute-start(bf16[4,2,2,2,2,32,128]{6,5,3,2,1,0,4:T(8,128)(2,1)S(1)} %maximum_bitcast_fusion), channel_id=1, source_target_pairs={{0,1},{1,0},{2,3},{3,2},{4,5},{5,4},{6,7},{7,6},{8,9},{9,8},{10,11... | collective-permute-start | bytes 1572872 | tf_op jit(solution)/shard_map/ppermute | solution.py:25
  54.6 2.1 %collective-permute-start.5 = (bf16[2,2,2,2,32,128]{5,4,2,1,0,3:T(8,128)(2,1)S(1)}, bf16[2,2,2,2,32,128]{5,4,2,1,0,3:T(8,128)(2,1)S(1)}, u32[]{:S(2)}, u32[]{:S(2)}) collective-permute-start(bf16[2,2,2,2,32,128]{5,4,2,1,0,3:T(8,128)(2,1)S(1)} %maximum_bitcast_fusion.1), channel_id=1, source_target_pairs={{0,1},{1,0},{2,3},{3,2},{4,5},{5,4},{6,7},{7,6},{8,9},{9,8},{10,11... | collective-permute-start | bytes 393224 | tf_op jit(solution)/shard_map/ppermute | solution.py:25
  56.9 1.2 %copy-start.1 = (bf16[1,4,1,4,2,128,128]{6,5,4,3,2,1,0:T(8,128)(2,1)S(1)}, bf16[1,4,1,4,2,128,128]{6,5,4,3,2,1,0:T(8,128)(2,1)}, u32[]{:S(2)}) copy-start(bf16[1,4,1,4,2,128,128]{6,5,4,3,2,1,0:T(8,128)(2,1)} %param.9) | copy-start | bytes 3145732
